TPU v7x, 256 devices: a whole 4x4x8 slice. The times are simulated.
256 devices in a mesh: ctx: 64 (over x, z, core), dp: 4 (over y).
Axes of the slice: x: 4, y: 4, z: 8, core: 2. Of those that a mesh axis runs over, the one named last changes fastest.
Arguments:
- queries: bfloat16 [65536, 128], P(('dp', 'ctx')), parts along dimension 0, may hold values from -12 to 12
- keys: bfloat16 [65536, 128], P(('dp', 'ctx')), parts along dimension 0, may hold values from -4 to 4
- values: bfloat16 [65536, 128], P(('dp', 'ctx')), parts along dimension 0, may hold values from -6 to 6
- out_grad: bfloat16 [65536, 128], P(('dp', 'ctx')), parts along dimension 0, may hold values from -6 to 6
- segments: int32 [65536], P(('dp', 'ctx')), parts along dimension 0, may hold values from 0 to 11, never falling along the last dimension, each value on 1 to 10240 neighbouring positions
Outputs:
- attended: bfloat16 [65536, 128], P(('dp', 'ctx')), parts along dimension 0
- query_grad: bfloat16 [65536, 128], P(('dp', 'ctx')), parts along dimension 0
- key_grad: bfloat16 [65536, 128], P(('dp', 'ctx')), parts along dimension 0
- value_grad: bfloat16 [65536, 128], P(('dp', 'ctx')), parts along dimension 0
There are 4 independent parts, one for each index of `dp`. A program takes and returns all parts, laid end to end along the dimension named above; each array names one. Nothing has to cross between parts.
Inputs may be any that keep to these rules, and one draw needn't show every extreme that they name: `segments`: ids never fall; every one of the 12 documents is present with 1 to 10240 tokens, one of exactly that many.
All inputs are finite; a program needn't handle non-finite values.
Results may differ from a plain program's by a relative error of at most 0.034.
Values may be sent and summed in bfloat16 or wider, within the bound.
A program may use at most 128 MiB of HBM per device.

v0:
```python
import math

import jax
import jax.numpy as jnp
from jax import lax
from jax.sharding import PartitionSpec as P

DOCS = 12


masked_score = -1e30


def swapped(block, axis, distance):
    count = lax.axis_size(axis)
    route = []
    for low in range(count):
        high = low | 1 << distance
        if high != low and high < count:
            route += [(low, high), (high, low)]
    return lax.ppermute(block, axis, route)


def per_device(queries, keys, values, out_grad, segments):
    tok_rows, head_width = queries.shape
    half_rows = tok_rows // 2
    cycle_size = lax.axis_size("ctx")
    bit_count = cycle_size.bit_length() - 1
    inv_root = 1.0 / math.sqrt(head_width)
    device_pos = lax.axis_index("ctx")
    labels = jnp.arange(DOCS, dtype=jnp.int32)
    one_hot = (segments[:, None] == labels[None, :]).astype(jnp.int32)
    counts = lax.psum(jnp.sum(one_hot, axis=0), "ctx")
    starts = jnp.cumsum(counts) - counts
    own_first = jnp.sum(one_hot * starts[None, :], axis=1)
    doc_end = own_first + jnp.sum(one_hot * counts[None, :], axis=1)
    own_pos = device_pos * tok_rows + jnp.arange(tok_rows, dtype=jnp.int32)
    partner = cycle_size - 1 - device_pos
    moving = jnp.stack([queries[half_rows:], out_grad[half_rows:]], axis=0)
    for bit in range(bit_count):
        moving = swapped(moving, "ctx", bit)
    q_rows = jnp.concatenate([queries[:half_rows], moving[0]], axis=0)
    g_rows = jnp.concatenate([out_grad[:half_rows], moving[1]], axis=0)
    query_pos = jnp.concatenate(
        [
            device_pos * tok_rows + jnp.arange(half_rows, dtype=jnp.int32),
            partner * tok_rows + half_rows + jnp.arange(half_rows, dtype=jnp.int32),
        ],
        axis=0,
    )
    row_first = jnp.max(
        jnp.where(starts[None, :] <= query_pos[:, None], starts[None, :], 0), axis=1
    )

    def query_mask(piece_len):
        key_pos = jnp.arange(piece_len, dtype=jnp.int32)
        return (key_pos[None, :] <= query_pos[:, None]) & (key_pos[None, :] >= row_first[:, None])

    key_piece = lax.all_gather(keys, "ctx", axis=0, tiled=True)
    value_piece = lax.all_gather(values, "ctx", axis=0, tiled=True)
    piece_len = key_piece.shape[0]
    run_max = jnp.full((tok_rows,), masked_score, jnp.float32)
    scores = (
        jnp.einsum("qd,kd->qk", q_rows, key_piece, preferred_element_type=jnp.float32) * inv_root
    )
    allowed = query_mask(piece_len)
    new_max = jnp.maximum(run_max, jnp.max(jnp.where(allowed, scores, masked_score), axis=1))
    exps = jnp.where(allowed, jnp.exp(scores - new_max[:, None]), 0.0)
    totals = jnp.sum(exps, axis=1)
    accum = jnp.dot(exps.astype(jnp.bfloat16), value_piece, preferred_element_type=jnp.float32)
    run_max, totals, accum = (new_max, totals, accum)
    attended_rows = (accum / totals[:, None]).astype(jnp.bfloat16)
    log_total = run_max + jnp.log(totals)
    row_delta = jnp.sum(g_rows.astype(jnp.float32) * attended_rows.astype(jnp.float32), axis=1)
    all_total, all_delta = (
        lax.all_gather(log_total, "ctx", axis=0, tiled=True),
        lax.all_gather(row_delta, "ctx", axis=0, tiled=True),
    )
    key_piece = lax.all_gather(keys, "ctx", axis=0, tiled=True)
    value_piece = lax.all_gather(values, "ctx", axis=0, tiled=True)
    piece_len = key_piece.shape[0]
    scores = (
        jnp.einsum("qd,kd->qk", q_rows, key_piece, preferred_element_type=jnp.float32) * inv_root
    )
    allowed = query_mask(piece_len)
    probs = jnp.where(allowed, jnp.exp(scores - log_total[:, None]), 0.0)
    prob_grad = jnp.einsum("qd,kd->qk", g_rows, value_piece, preferred_element_type=jnp.float32)
    score_grad = (probs * (prob_grad - row_delta[:, None]) * inv_root).astype(jnp.bfloat16)
    query_sum = jnp.dot(score_grad, key_piece, preferred_element_type=jnp.float32)
    query_rows_grad = query_sum.astype(jnp.bfloat16)
    returning = jnp.stack([attended_rows[half_rows:], query_rows_grad[half_rows:]], axis=0)
    for bit in range(bit_count):
        returning = swapped(returning, "ctx", bit)
    attended = jnp.concatenate([attended_rows[:half_rows], returning[0]], axis=0)
    query_grad = jnp.concatenate([query_rows_grad[:half_rows], returning[1]], axis=0)
    query_piece = lax.all_gather(q_rows, "ctx", axis=0, tiled=True)
    grad_piece = lax.all_gather(g_rows, "ctx", axis=0, tiled=True)
    piece_len = query_piece.shape[0]
    piece_index = jnp.arange(piece_len, dtype=jnp.int32)
    source_dev = piece_index // tok_rows
    within = piece_index % tok_rows
    piece_pos = jnp.where(
        within < half_rows,
        source_dev * tok_rows + within,
        (cycle_size - 1 - source_dev) * tok_rows + within,
    )
    scores = (
        jnp.einsum("qd,kd->qk", query_piece, keys, preferred_element_type=jnp.float32) * inv_root
    )
    allowed = (piece_pos[:, None] >= own_pos[None, :]) & (piece_pos[:, None] < doc_end[None, :])
    probs = jnp.where(allowed, jnp.exp(scores - all_total[:, None]), 0.0)
    value_acc = jnp.einsum(
        "qk,qd->kd", probs.astype(jnp.bfloat16), grad_piece, preferred_element_type=jnp.float32
    )
    prob_grad = jnp.einsum("qd,kd->qk", grad_piece, values, preferred_element_type=jnp.float32)
    score_grad = (probs * (prob_grad - all_delta[:, None]) * inv_root).astype(jnp.bfloat16)
    key_acc = jnp.einsum("qk,qd->kd", score_grad, query_piece, preferred_element_type=jnp.float32)
    return (attended, query_grad, key_acc.astype(jnp.bfloat16), value_acc.astype(jnp.bfloat16))


def solution(mesh):
    placed = (
        P(("dp", "ctx"), None),
        P(("dp", "ctx"), None),
        P(("dp", "ctx"), None),
        P(("dp", "ctx"), None),
        P(("dp", "ctx")),
    )
    return jax.shard_map(
        per_device,
        mesh=mesh,
        in_specs=placed,
        out_specs=(
            P(("dp", "ctx"), None),
            P(("dp", "ctx"), None),
            P(("dp", "ctx"), None),
            P(("dp", "ctx"), None),
        ),
        check_vma=False,
    )
```

profile of v0, /device:TPU:8, one launch (start us, length us, event | category | flops | bytes accessed | tf_op | source)
XLA Modules:
  0.0 364.0 jit_solution(4180193362576359597)
XLA Ops:
  11.6 1.9 collective-permute-start.1
  13.5 2.4 collective-permute-done.1
  15.9 3.3 collective-permute-start.2
  19.2 2.6 collective-permute-done.2
  21.8 7.3 %collective-permute-start.3 = (bf16[2,128,128]{2,1,0:T(8,128)(2,1)S(1)}, bf16[2,128,128]{2,1,0:T(8,128)(2,1)S(1)}, u32[]{:S(2)}, u32[]{:S(2)}) collective-permute-start(bf16[2,128,128]{2,1,0:T(8,128)(2,1)S(1)} %collective-permute-done.2), channel_id=1, source_target_pairs={{0,32},{32,0},{4,36},{36,4},{8,40},{40,8},{12,44},{44,12},{16,48},... | collective-permute-start | bytes 196616 | tf_op jit(solution)/shard_map/ppermute | solution.py:21
  29.0 2.3 collective-permute-done.3
  31.3 1.5 collective-permute-start.4
  32.8 2.8 collective-permute-done.4
  35.7 3.7 %collective-permute-start.5 = (bf16[2,128,128]{2,1,0:T(8,128)(2,1)S(1)}, bf16[2,128,128]{2,1,0:T(8,128)(2,1)S(1)}, u32[]{:S(2)}, u32[]{:S(2)}) collective-permute-start(bf16[2,128,128]{2,1,0:T(8,128)(2,1)S(1)} %collective-permute-done.4), channel_id=1, source_target_pairs={{0,128},{128,0},{4,132},{132,4},{8,136},{136,8},{12,140},{140,12},... | collective-permute-start | bytes 196616 | tf_op jit(solution)/shard_map/ppermute | solution.py:21
  39.4 2.3 collective-permute-done.5
  43.2 22.2 %psum.7 = s32[12]{0:T(128)S(1)} all-reduce(s32[12]{0:T(128)S(1)} %convert_reduce_fusion), channel_id=1, replica_groups=mesh['ctx'=64,'dp'=4] {'ctx'}, use_global_device_ids=true, to_apply=%region_1.0 | all-reduce | flops 12 | bytes 96 | tf_op jit(solution)/shard_map/psum | solution.py:33
  67.1 25.6 %all-gather.7.cloned.1.call-done = bf16[16384,128]{1,0:T(8,128)(2,1)} async-done(((bf16[256,128]{1,0:T(8,128)(2,1)}), bf16[16384,128]{1,0:T(8,128)(2,1)}) %all-gather.7.cloned.1.call-update) | async-done | bytes 4194320 | tf_op jit(solution)/shard_map/all_gather | solution.py:59
  92.7 7.1 %select_reduce_fusion = (f32[256]{0:T(256)S(1)}, f32[256,16384]{1,0:T(8,128)S(1)}) fusion(s32[256]{0:T(256)S(1)} %get-tuple-element.6, s32[256]{0:T(256)S(1)} %pad_add_fusion, bf16[16384,128]{1,0:T(8,128)(2,1)} %all-gather.7.cloned.1.call-done, bf16[128,128]{1,0:T(8,128)(2,1)S(1)} %get-tuple-element.16, bf16[128,128]{1,0:T(8,128)(2,1)S(1)} %get-tuple-element.17), kind=kOutput, calls=%fused_computation.14 | convolution fusion | flops 1099038464 | bytes 21040128 | tf_op jit(solution)/shard_map/qd,kd->qk/dot_general | solution.py:64
  99.8 5.7 %copy-done = f32[256,16384]{1,0:T(8,128)} copy-done((f32[256,16384]{1,0:T(8,128)}, f32[256,16384]{1,0:T(8,128)S(1)}, u32[]{:S(2)}) %copy-start) | copy-done | bytes 16777240
  105.5 6.0 %fusion.10 = f32[256]{0:T(256)S(1)} fusion(f32[256,16384]{1,0:T(8,128)S(1)} %get-tuple-element.20, f32[256]{0:T(256)S(1)} %broadcast_maximum_fusion, s32[256]{0:T(256)S(1)} %get-tuple-element.6, s32[256]{0:T(256)S(1)} %pad_add_fusion), kind=kLoop, calls=%fused_computation.18 | loop fusion | flops 25165568 | bytes 16781312 | tf_op jit(solution)/shard_map/reduce_sum | solution.py:69
  111.5 60.3 %all-gather.9.cloned.1.call-done = bf16[16384,128]{1,0:T(8,128)(2,1)} async-done(((bf16[256,128]{1,0:T(8,128)(2,1)}), bf16[16384,128]{1,0:T(8,128)(2,1)}) %all-gather.9.cloned.1.call-update) | async-done | bytes 4194320 | tf_op jit(solution)/shard_map/all_gather | solution.py:60
  171.8 10.4 %multiply_reduce_fusion = (f32[256]{0:T(256)S(1)}, bf16[256,128]{1,0:T(8,128)(2,1)S(1)}) fusion(bf16[128,128]{1,0:T(8,128)(2,1)S(1)} %get-tuple-element.15, bf16[128,128]{1,0:T(8,128)(2,1)S(1)} %get-tuple-element.13, f32[256]{0:T(256)S(1)} %fusion.10, bf16[16384,128]{1,0:T(8,128)(2,1)} %all-gather.9.cloned.1.call-done, f32[256,16384]{1,0:T(8,128)} %copy-done, ...), kind=kOutput, calls=%fused_computation.39 | convolution fusion | flops 1099202304 | bytes 21107712 | tf_op jit(solution)/shard_map/dot_general | solution.py:70
  182.2 17.1 %fusion.22 = bf16[256,128]{1,0:T(8,128)(2,1)S(1)} fusion(bf16[16384,128]{1,0:T(8,128)(2,1)} %all-gather.7.cloned.1.call-done, bf16[16384,128]{1,0:T(8,128)(2,1)} %all-gather.9.cloned.1.call-done, f32[256,16384]{1,0:T(8,128)} %copy-done, f32[256]{0:T(256)S(1)} %get-tuple-element.21, f32[256]{0:T(256)S(1)} %log_add_fusion, s32[256]{0:T(256)S(1)} %get-tuple-element.6, ...), kind=kOutput, calls=%fused_computation.28 | convolution fusion | flops 2185396224 | bytes 25300992 | tf_op jit(solution)/shard_map/dot_general | solution.py:89
  201.5 3.7 %collective-permute-done.7 = bf16[2,128,128]{2,1,0:T(8,128)(2,1)S(1)} collective-permute-done((bf16[2,128,128]{2,1,0:T(8,128)(2,1)S(1)}, bf16[2,128,128]{2,1,0:T(8,128)(2,1)S(1)}, u32[]{:S(2)}, u32[]{:S(2)}) %collective-permute-start.7) | collective-permute-done | bytes 65568 | tf_op jit(solution)/shard_map/ppermute | solution.py:21
  205.2 2.1 collective-permute-start.8
  207.3 3.9 %collective-permute-done.8 = bf16[2,128,128]{2,1,0:T(8,128)(2,1)S(1)} collective-permute-done((bf16[2,128,128]{2,1,0:T(8,128)(2,1)S(1)}, bf16[2,128,128]{2,1,0:T(8,128)(2,1)S(1)}, u32[]{:S(2)}, u32[]{:S(2)}) %collective-permute-start.8) | collective-permute-done | bytes 65568 | tf_op jit(solution)/shard_map/ppermute | solution.py:21
  211.2 3.0 collective-permute-start.9
  214.2 5.2 %collective-permute-done.9 = bf16[2,128,128]{2,1,0:T(8,128)(2,1)S(1)} collective-permute-done((bf16[2,128,128]{2,1,0:T(8,128)(2,1)S(1)}, bf16[2,128,128]{2,1,0:T(8,128)(2,1)S(1)}, u32[]{:S(2)}, u32[]{:S(2)}) %collective-permute-start.9) | collective-permute-done | bytes 65568 | tf_op jit(solution)/shard_map/ppermute | solution.py:21
  219.4 1.4 collective-permute-start.10
  220.9 3.7 %collective-permute-done.10 = bf16[2,128,128]{2,1,0:T(8,128)(2,1)S(1)} collective-permute-done((bf16[2,128,128]{2,1,0:T(8,128)(2,1)S(1)}, bf16[2,128,128]{2,1,0:T(8,128)(2,1)S(1)}, u32[]{:S(2)}, u32[]{:S(2)}) %collective-permute-start.10) | collective-permute-done | bytes 65568 | tf_op jit(solution)/shard_map/ppermute | solution.py:21
  224.6 3.0 collective-permute-start.11
  227.6 42.3 %all-gather = f32[64,1,256]{2,1,0:T(1,128)S(1)} all-gather(f32[1,1,256]{2,1,0:T(1,128)S(1)} %bitcast.35), channel_id=1, replica_groups=mesh['ctx'=64,'dp'=4] {'ctx'}, dimensions={0}, use_global_device_ids=true | all-gather | bytes 66560 | tf_op jit(solution)/shard_map/all_gather | solution.py:76
  269.8 42.1 %all-gather.1 = f32[64,1,256]{2,1,0:T(1,128)S(1)} all-gather(f32[1,1,256]{2,1,0:T(1,128)S(1)} %bitcast.36), channel_id=1, replica_groups=mesh['ctx'=64,'dp'=4] {'ctx'}, dimensions={0}, use_global_device_ids=true | all-gather | bytes 66560 | tf_op jit(solution)/shard_map/all_gather | solution.py:77
  313.2 13.5 %fusion.8 = f32[16384,256]{1,0:T(8,128)} fusion(bf16[16384,128]{1,0:T(8,128)(2,1)} %all-gather.11.cloned.1.call-done, bf16[256,128]{1,0:T(8,128)(2,1)S(1)} %copy-done.2, f32[16384]{0:T(1024)S(1)} %bitcast.34, s32[256]{0:T(256)S(1)} %add.87, s32[256]{0:T(256)S(1)} %iota_add_fusion, s32[16384]{0:T(1024)S(1)} %fusion.41), kind=kOutput, calls=%fused_computation.12 | convolution fusion | flops 1098907648 | bytes 21170176 | tf_op jit(solution)/shard_map/qd,kd->qk/dot_general | solution.py:108
  326.7 4.4 %all-gather.13.cloned.1.call-done = bf16[16384,128]{1,0:T(8,128)(2,1)} async-done(((bf16[256,128]{1,0:T(8,128)(2,1)}), bf16[16384,128]{1,0:T(8,128)(2,1)}) %all-gather.13.cloned.1.call-update) | async-done | bytes 4194320 | tf_op jit(solution)/shard_map/all_gather | solution.py:97
  331.1 10.0 %fusion.23 = bf16[256,128]{1,0:T(8,128)(2,1)} fusion(bf16[16384,128]{1,0:T(8,128)(2,1)} %all-gather.13.cloned.1.call-done, f32[16384,256]{1,0:T(8,128)} %fusion.8), kind=kOutput, calls=%fused_computation.29 | convolution fusion | flops 1077968896 | bytes 21037056 | tf_op jit(solution)/shard_map/qk,qd->kd/dot_general | solution.py:112
  341.1 16.4 %fusion.21 = bf16[256,128]{1,0:T(8,128)(2,1)} fusion(bf16[16384,128]{1,0:T(8,128)(2,1)} %all-gather.11.cloned.1.call-done, f32[16384,256]{1,0:T(8,128)} %fusion.8, bf16[16384,128]{1,0:T(8,128)(2,1)} %all-gather.13.cloned.1.call-done, bf16[256,128]{1,0:T(8,128)(2,1)S(1)} %copy-done.1, f32[16384]{0:T(1024)S(1)} %bitcast.33), kind=kOutput, calls=%fused_computation.27 | convolution fusion | flops 2164293632 | bytes 25362432 | tf_op jit(solution)/shard_map/qk,qd->kd/dot_general | solution.py:117
  (43 shorter events, 11.0 us)
Async XLA Ops:
  7.2 85.5 %all-gather.7.cloned.1.call-start = ((), (), s32[]{:S(2)}) async-start(), calls=%async_computation | async-start | bytes 4259840 | tf_op jit(solution)/shard_map/all_gather | solution.py:59
  7.9 163.9 %all-gather.9.cloned.1.call-start = ((), (), s32[]{:S(2)}) async-start(), calls=%async_computation.1 | async-start | bytes 4259840 | tf_op jit(solution)/shard_map/all_gather | solution.py:60
  8.6 304.5 %all-gather.11.cloned.1.call-start = ((), (), s32[]{:S(2)}) async-start(), calls=%async_computation.2 | async-start | bytes 4259840 | tf_op jit(solution)/shard_map/all_gather | solution.py:96
  10.3 1.3 collective-permute-start
  11.6 4.3 %collective-permute-start.1 = (bf16[2,128,128]{2,1,0:T(8,128)(2,1)S(1)}, bf16[2,128,128]{2,1,0:T(8,128)(2,1)S(1)}, u32[]{:S(2)}, u32[]{:S(2)}) collective-permute-start(bf16[2,128,128]{2,1,0:T(8,128)(2,1)S(1)} %collective-permute-done), channel_id=1, source_target_pairs={{0,8},{8,0},{4,12},{12,4},{16,24},{24,16},{20,28},{28,20},{32,40},... | collective-permute-start | bytes 196616 | tf_op jit(solution)/shard_map/ppermute | solution.py:21
  15.9 5.8 %collective-permute-start.2 = (bf16[2,128,128]{2,1,0:T(8,128)(2,1)S(1)}, bf16[2,128,128]{2,1,0:T(8,128)(2,1)S(1)}, u32[]{:S(2)}, u32[]{:S(2)}) collective-permute-start(bf16[2,128,128]{2,1,0:T(8,128)(2,1)S(1)} %collective-permute-done.1), channel_id=1, source_target_pairs={{0,16},{16,0},{4,20},{20,4},{8,24},{24,8},{12,28},{28,12},{32,48},... | collective-permute-start | bytes 196616 | tf_op jit(solution)/shard_map/ppermute | solution.py:21
  21.8 9.6 %collective-permute-start.3 = (bf16[2,128,128]{2,1,0:T(8,128)(2,1)S(1)}, bf16[2,128,128]{2,1,0:T(8,128)(2,1)S(1)}, u32[]{:S(2)}, u32[]{:S(2)}) collective-permute-start(bf16[2,128,128]{2,1,0:T(8,128)(2,1)S(1)} %collective-permute-done.2), channel_id=1, source_target_pairs={{0,32},{32,0},{4,36},{36,4},{8,40},{40,8},{12,44},{44,12},{16,48},... | collective-permute-start | bytes 196616 | tf_op jit(solution)/shard_map/ppermute | solution.py:21
  31.3 4.3 %collective-permute-start.4 = (bf16[2,128,128]{2,1,0:T(8,128)(2,1)S(1)}, bf16[2,128,128]{2,1,0:T(8,128)(2,1)S(1)}, u32[]{:S(2)}, u32[]{:S(2)}) collective-permute-start(bf16[2,128,128]{2,1,0:T(8,128)(2,1)S(1)} %collective-permute-done.3), channel_id=1, source_target_pairs={{0,64},{64,0},{4,68},{68,4},{8,72},{72,8},{12,76},{76,12},{16,80},... | collective-permute-start | bytes 196616 | tf_op jit(solution)/shard_map/ppermute | solution.py:21
  35.7 6.0 %collective-permute-start.5 = (bf16[2,128,128]{2,1,0:T(8,128)(2,1)S(1)}, bf16[2,128,128]{2,1,0:T(8,128)(2,1)S(1)}, u32[]{:S(2)}, u32[]{:S(2)}) collective-permute-start(bf16[2,128,128]{2,1,0:T(8,128)(2,1)S(1)} %collective-permute-done.4), channel_id=1, source_target_pairs={{0,128},{128,0},{4,132},{132,4},{8,136},{136,8},{12,140},{140,12},... | collective-permute-start | bytes 196616 | tf_op jit(solution)/shard_map/ppermute | solution.py:21
  42.4 288.7 %all-gather.13.cloned.1.call-start = ((), (), s32[]{:S(2)}) async-start(), calls=%async_computation.3 | async-start | bytes 4259840 | tf_op jit(solution)/shard_map/all_gather | solution.py:97
  99.8 5.7 %copy-start = (f32[256,16384]{1,0:T(8,128)}, f32[256,16384]{1,0:T(8,128)S(1)}, u32[]{:S(2)}) copy-start(f32[256,16384]{1,0:T(8,128)S(1)} %get-tuple-element.20) | copy-start | bytes 50331652
  182.2 131.0 %copy-start.2 = (bf16[256,128]{1,0:T(8,128)(2,1)S(1)}, bf16[256,128]{1,0:T(8,128)(2,1)}, u32[]{:S(2)}) copy-start(bf16[256,128]{1,0:T(8,128)(2,1)} %param.6) | copy-start | bytes 196612
  199.4 1.3 collective-permute-start.6
  200.7 4.5 %collective-permute-start.7 = (bf16[2,128,128]{2,1,0:T(8,128)(2,1)S(1)}, bf16[2,128,128]{2,1,0:T(8,128)(2,1)S(1)}, u32[]{:S(2)}, u32[]{:S(2)}) collective-permute-start(bf16[2,128,128]{2,1,0:T(8,128)(2,1)S(1)} %collective-permute-done.6), channel_id=1, source_target_pairs={{0,8},{8,0},{4,12},{12,4},{16,24},{24,16},{20,28},{28,20},{32,40},... | collective-permute-start | bytes 196616 | tf_op jit(solution)/shard_map/ppermute | solution.py:21
  205.2 6.0 %collective-permute-start.8 = (bf16[2,128,128]{2,1,0:T(8,128)(2,1)S(1)}, bf16[2,128,128]{2,1,0:T(8,128)(2,1)S(1)}, u32[]{:S(2)}, u32[]{:S(2)}) collective-permute-start(bf16[2,128,128]{2,1,0:T(8,128)(2,1)S(1)} %collective-permute-done.7), channel_id=1, source_target_pairs={{0,16},{16,0},{4,20},{20,4},{8,24},{24,8},{12,28},{28,12},{32,48},... | collective-permute-start | bytes 196616 | tf_op jit(solution)/shard_map/ppermute | solution.py:21
  211.2 8.2 %collective-permute-start.9 = (bf16[2,128,128]{2,1,0:T(8,128)(2,1)S(1)}, bf16[2,128,128]{2,1,0:T(8,128)(2,1)S(1)}, u32[]{:S(2)}, u32[]{:S(2)}) collective-permute-start(bf16[2,128,128]{2,1,0:T(8,128)(2,1)S(1)} %collective-permute-done.8), channel_id=1, source_target_pairs={{0,32},{32,0},{4,36},{36,4},{8,40},{40,8},{12,44},{44,12},{16,48},... | collective-permute-start | bytes 196616 | tf_op jit(solution)/shard_map/ppermute | solution.py:21
  219.4 5.2 %collective-permute-start.10 = (bf16[2,128,128]{2,1,0:T(8,128)(2,1)S(1)}, bf16[2,128,128]{2,1,0:T(8,128)(2,1)S(1)}, u32[]{:S(2)}, u32[]{:S(2)}) collective-permute-start(bf16[2,128,128]{2,1,0:T(8,128)(2,1)S(1)} %collective-permute-done.9), channel_id=1, source_target_pairs={{0,64},{64,0},{4,68},{68,4},{8,72},{72,8},{12,76},{76,12},{16,80},... | collective-permute-start | bytes 196616 | tf_op jit(solution)/shard_map/ppermute | solution.py:21
  224.6 87.3 %collective-permute-start.11 = (bf16[2,128,128]{2,1,0:T(8,128)(2,1)S(1)}, bf16[2,128,128]{2,1,0:T(8,128)(2,1)S(1)}, u32[]{:S(2)}, u32[]{:S(2)}) collective-permute-start(bf16[2,128,128]{2,1,0:T(8,128)(2,1)S(1)} %collective-permute-done.10), channel_id=1, source_target_pairs={{0,128},{128,0},{4,132},{132,4},{8,136},{136,8},{12,140},{140,12},... | collective-permute-start | bytes 196616 | tf_op jit(solution)/shard_map/ppermute | solution.py:21
  326.7 14.4 %copy-start.1 = (bf16[256,128]{1,0:T(8,128)(2,1)S(1)}, bf16[256,128]{1,0:T(8,128)(2,1)}, u32[]{:S(2)}) copy-start(bf16[256,128]{1,0:T(8,128)(2,1)} %param.7) | copy-start | bytes 196612
Sparse Core Ops, SparseCore 0:
  10.8 81.8 all-gather.6
  95.5 76.2 all-gather.8
  175.1 76.6 all-gather.10
  255.0 76.0 all-gather.12
where the time goes:
time: 366 us; the launch traced here: 364 us
  waiting for transfers between devices  123 us (34%)
  blocking collectives  107 us (29%)
  matrix products  74.6 us (20%)
  starting transfers between devices  28.6 us (8%)
  between operations  13.9 us (4%)
  other arithmetic  10.3 us (3%)
  local copies, waits for them, and re-layouts  7.32 us (2%)
    all_gather x1, waiting for transfers between devices, per_device(): value_piece = lax.all_gather(values, 'ctx', axis=0, tiled=True)  60.3 us
    all_gather x1, blocking collectives, per_device(): lax.all_gather(log_total, 'ctx', axis=0, tiled=True)  42.3 us
    all_gather x1, blocking collectives, per_device(): lax.all_gather(row_delta, 'ctx', axis=0, tiled=True)  42.1 us
    ppermute x12, waiting for transfers between devices, swapped(): return lax.ppermute(block, axis, route)  31.2 us
    ppermute x12, starting transfers between devices, swapped(): return lax.ppermute(block, axis, route)  28.4 us
    all_gather x1, waiting for transfers between devices, per_device(): key_piece = lax.all_gather(keys, 'ctx', axis=0, tiled=True)  25.6 us
    psum x1, blocking collectives, per_device(): counts = lax.psum(jnp.sum(one_hot, axis=0), 'ctx')  22.2 us
    dot_general x1, matrix products, per_device(): jnp.dot(score_grad, key_piece, preferred_element_type=jnp.float32)  17.1 us
  transfers between devices with their start and end apart: 16, of which 14 were waited for; matrix products, arithmetic and copies ran while one was open for 17% of the time, Pallas kernels for 0%

commit v1 on v0

v1 whole, which is shorter than its diff:
```python
import functools
import math

import jax
import jax.numpy as jnp
from jax import lax
from jax.experimental import pallas as pl
from jax.experimental.pallas import tpu as pltpu
from jax.sharding import PartitionSpec as P

MESH = pl.DeviceIdType.MESH
HD = 128
X, Z = 4, 8
T = 256
C = 2 * T
SEG_ROWS = 16
NEG = -1e30
INV_ROOT = 1.0 / math.sqrt(HD)
ALPHA = INV_ROOT * math.log2(math.e)
F32 = jnp.float32
BF16 = jnp.bfloat16
NT = (((1,), (1,)), ((), ()))


def kernel(
    q_ref, k_ref, v_ref, g_ref, seg_ref,
    att_ref, dq_ref, dk_ref, dv_ref,
    qs, gs, ks, vs, kt, vt, eb, dp, pb, db, acc, kacc, cnt,
    sts, str_, fin, zs, zr, sbs, sbr, xs, xr,
    zq_s, zq_r, zg_s, zg_r, kv_s, kv_r, st_s, st_r, fn_s, fn_r,
    za_s, za_r, sb_s, sb_r, xr_s, xr_r,
):
    ctx = lax.axis_index("ctx")
    x = ctx // (2 * Z)
    z = (ctx // 2) % Z
    core = ctx % 2

    def dev(xx, zz, cc):
        return {"ctx": ((xx + X) % X) * (2 * Z) + ((zz + Z) % Z) * 2 + cc}

    sib = dev(x, z, 1 - core)
    z_right, z_left = dev(x, z + 1, core), dev(x, z - 1, core)
    x_right, x_left = dev(x + 1, z, core), dev(x - 1, z, core)

    barrier = pltpu.get_barrier_semaphore()
    for r in range(1, Z):
        pl.semaphore_signal(barrier, inc=1, device_id=dev(x, z - r, core), device_id_type=MESH)
    for peer in (sib, x_right, x_left):
        pl.semaphore_signal(barrier, inc=1, device_id=peer, device_id_type=MESH)

    qs[0, 0:T, :] = q_ref[...]
    qs[0, T : T + SEG_ROWS, :] = seg_ref[...]
    gs[0] = g_ref[...]
    ks[0, core, 0:T, :] = k_ref[...]
    ks[0, core, T : T + SEG_ROWS, :] = seg_ref[...]
    vs[0, core] = v_ref[...]

    pl.semaphore_wait(barrier, Z + 2)

    started = []

    def copy(src, dst, send, recv, target):
        return pltpu.make_async_remote_copy(
            src_ref=src, dst_ref=dst, send_sem=send, recv_sem=recv,
            device_id=target, device_id_type=MESH,
        )

    def send(op):
        op.start()
        started.append(op)

    def q_hop(src, dst, target):
        return copy(qs.at[src], qs.at[dst], zq_s.at[dst], zq_r.at[dst], target)

    def g_hop(src, dst, target):
        return copy(gs.at[src], gs.at[dst], zg_s.at[dst], zg_r.at[dst], target)

    def k_hop(i, src, dst, target):
        return copy(ks.at[src, core], ks.at[dst, core], kv_s.at[i], kv_r.at[i], target)

    def v_hop(i, src, dst, target):
        return copy(vs.at[src, core], vs.at[dst, core], kv_s.at[i], kv_r.at[i], target)

    q_right = [q_hop(j, j + 1, z_right) for j in range(4)]
    q_left = [q_hop((8 - j) % 8, 7 - j, z_left) for j in range(3)]
    g_right = [g_hop(j, j + 1, z_right) for j in range(3)]
    g_left = [g_hop((8 - j) % 8, 7 - j, z_left) for j in range(4)]
    k_sib = {0: k_hop(0, 0, 0, sib), 1: k_hop(1, 1, 1, sib), 2: k_hop(2, 2, 2, sib), 3: k_hop(3, 3, 3, sib)}
    v_sib = {0: v_hop(4, 0, 0, sib), 1: v_hop(5, 1, 1, sib), 2: v_hop(6, 2, 2, sib), 3: v_hop(7, 3, 3, sib)}
    k_right, v_right = k_hop(8, 0, 1, x_right), v_hop(9, 0, 1, x_right)
    k_left, v_left = k_hop(10, 0, 3, x_left), v_hop(11, 0, 3, x_left)
    k_far, v_far = k_hop(12, 1, 2, x_right), v_hop(13, 3, 2, x_left)

    for op in (q_right[0], q_left[0], k_right, k_left, g_right[0], g_left[0], v_right, v_left, k_sib[0], v_sib[0]):
        send(op)

    def z_step(j):
        q_right[j - 1].wait_recv()
        if j < 4:
            q_right[j].start()
            q_left[j - 1].wait_recv()
        if j < 3:
            q_left[j].start()
        g_left[j - 1].wait_recv()
        if j < 4:
            g_left[j].start()
            g_right[j - 1].wait_recv()
        if j < 3:
            g_right[j].start()

    z_step(1)
    k_right.wait_recv()
    send(k_far)
    send(k_sib[1])
    v_left.wait_recv()
    send(v_far)
    send(v_sib[3])
    v_right.wait_recv()
    send(v_sib[1])
    k_left.wait_recv()
    send(k_sib[3])
    k_far.wait_recv()
    send(k_sib[2])
    v_far.wait_recv()
    send(v_sib[2])
    for s in range(X):
        k_sib[s].wait_recv()
        v_sib[s].wait_recv()
    z_step(2)

    doc16 = lax.broadcasted_iota(jnp.int32, (16, HD), 0).astype(F32)

    def prepare(s, _):
        below = jnp.zeros((16, HD), F32)
        for c in range(2):
            kt[s, :, c * T : (c + 1) * T] = ks[s, c, 0:T, :].T
            vt[s, :, c * T : (c + 1) * T] = vs[s, c].T
            seg = ks[s, c, T : T + SEG_ROWS, :].astype(F32)
            for h in range(T // HD):
                below += jnp.where(seg[h : h + 1, :] < doc16, 1.0, 0.0)
        cnt[s] = jnp.broadcast_to(jnp.sum(below, axis=1, keepdims=True), (16, T))
        return 0

    lax.fori_loop(0, X, prepare, 0)

    def slots(r):
        own = (r == 0) | (r > z)
        used = own | ((x == X - 1) & (r >= 4))
        return jnp.where(used, 0, 1), jnp.where(own, 0, 3), jnp.minimum(x, 2) + 1

    key_row = lax.broadcasted_iota(jnp.int32, (T, T), 0).astype(F32)
    query_lane = lax.broadcasted_iota(jnp.int32, (1, T), 1).astype(F32)
    doc_q = lax.broadcasted_iota(jnp.int32, (16, T), 0).astype(F32)

    def stat_send(r):
        return copy(sts.at[r], str_.at[r], st_s.at[r], st_r.at[r], dev(x, z - r, core))

    def first(i, _):
        @pl.when(i == 3)
        def _():
            z_step(3)

        @pl.when(i == 5)
        def _():
            z_step(4)

        r = jnp.where(i % 2 == 1, (i + 1) // 2, (8 - i // 2) % 8)
        u_low, s_zero, u_high = slots(r)
        seg = qs[r, T : T + SEG_ROWS, :].astype(F32)
        seg_q = jnp.concatenate([seg[0:1, :], seg[1:2, :]], axis=1)
        same = seg_q == doc_q

        def scores(u, top):
            s = jnp.where(u == 0, s_zero, u)
            low = jnp.sum(jnp.where(same, cnt[s], 0.0), axis=0, keepdims=True)
            diagonal = (s == 0) & (r == 0)
            high = jnp.where(diagonal, query_lane + (core * T).astype(F32), 1e9)
            for c in range(2):
                sc = lax.dot_general(ks[s, c, 0:T, :], qs[r, 0:T, :], NT, preferred_element_type=F32)
                pos = key_row + c * T
                sc = jnp.where((pos >= low) & (pos <= high), sc, NEG)
                eb[r, u, c * T : (c + 1) * T, :] = sc
                top = jnp.maximum(top, jnp.max(sc, axis=0, keepdims=True))
            return top

        top = lax.fori_loop(u_low, u_high, scores, jnp.full((1, T), NEG, F32))

        def exps(u, sums):
            total, moment = sums
            s = jnp.where(u == 0, s_zero, u)
            for c in range(2):
                rows = slice(c * T, (c + 1) * T)
                e = jnp.exp2((eb[r, u, rows, :] - top) * ALPHA)
                eb[r, u, rows, :] = e
                grad = lax.dot_general(vs[s, c], gs[r], NT, preferred_element_type=F32)
                dp[r, u, rows, :] = grad
                total += jnp.sum(e, axis=0, keepdims=True)
                moment += jnp.sum(e * grad, axis=0, keepdims=True)
            return total, moment

        zero = jnp.zeros((1, T), F32)
        total, moment = lax.fori_loop(u_low, u_high, exps, (zero, zero))
        sts[r, 0:1, :] = top
        sts[r, 1:2, :] = total
        sts[r, 2:3, :] = moment

        @pl.when(i > 0)
        def _():
            stat_send(r).start()

        return 0

    lax.fori_loop(0, Z, first, 0)

    for r in range(1, Z):
        stat_send(r).wait_recv()
    tops = [sts[0, 0:1, :]] + [str_[r, 0:1, :] for r in range(1, Z)]
    top = functools.reduce(jnp.maximum, tops)
    total = jnp.zeros((1, T), F32)
    moment = jnp.zeros((1, T), F32)
    for r in range(Z):
        box = sts if r == 0 else str_
        scale = jnp.exp2((tops[r] - top) * ALPHA)
        total += box[r, 1:2, :] * scale
        moment += box[r, 2:3, :] * scale
    inverse = 1.0 / total
    fin[0, 0:1, :] = top
    fin[0, 1:2, :] = inverse
    fin[0, 2:3, :] = moment * inverse

    def fin_send(r):
        return copy(fin.at[0], fin.at[r], fn_s.at[r], fn_r.at[r], dev(x, z + r, core))

    for r in (4, 3, 5, 2, 6, 1, 7):
        send(fin_send(r))

    def z_sum(d, i, what):
        return copy(
            zs.at[d, i, what], zr.at[d, i, what], za_s.at[d, i, what], za_r.at[d, i, what],
            z_right if d == 0 else z_left,
        )

    def z_add(i):
        for d in range(2):
            r = 4 + i if d == 0 else 4 - i
            for what in range(2):
                part = acc[r, what]
                if i > 1 or what == d:
                    z_sum(d, i - 1, what).wait_recv()
                    part = part + zr[d, i - 1, what].astype(F32)
                zs[d, i, what] = part.astype(BF16)
                send(z_sum(d, i, what))

    def second(i, _):
        @pl.when(i == 1)
        def _():
            for d in range(2):
                zs[d, 0, d] = acc[4, d].astype(BF16)
                z_sum(d, 0, d).start()

        r = jnp.where(i % 2 == 1, (4 + (i + 1) // 2) % 8, 4 - i // 2)

        @pl.when(r > 0)
        def _():
            fin_send(r).wait_recv()

        u_low, s_zero, u_high = slots(r)
        scale = jnp.exp2((sts[r, 0:1, :] - fin[r, 0:1, :]) * ALPHA) * fin[r, 1:2, :]
        delta = fin[r, 2:3, :]
        root_scale = scale * INV_ROOT
        acc[r] = jnp.zeros((2, HD, T), F32)
        lanes = pl.ds(pl.multiple_of(r * T, T), T)

        def body(u, _):
            s = jnp.where(u == 0, s_zero, u)
            e = eb[r, u]
            p = (e * scale).astype(BF16)
            ds = (e * root_scale * (dp[r, u] - delta)).astype(BF16)
            pb[u, :, lanes] = p
            db[u, :, lanes] = ds
            acc[r, 0] += jnp.dot(vt[s], p, preferred_element_type=F32)
            acc[r, 1] += jnp.dot(kt[s], ds, preferred_element_type=F32)
            return 0

        lax.fori_loop(u_low, u_high, body, 0)
        return 0

    lax.fori_loop(0, Z, second, 0)
    z_add(1)

    def sib_send(s):
        return copy(sbs.at[s], sbr.at[s], sb_s.at[s], sb_r.at[s], sib)

    def key_part(s, u, r_low, r_high):
        kacc[s] = jnp.zeros((2, C, HD), F32)

        def body(i, _):
            r = i % Z
            lanes = pl.ds(pl.multiple_of(r * T, T), T)
            kacc[s, 0] += jnp.dot(db[u, :, lanes], qs[r, 0:T, :], preferred_element_type=F32)
            kacc[s, 1] += jnp.dot(pb[u, :, lanes], gs[r], preferred_element_type=F32)
            return 0

        lax.fori_loop(r_low, r_high, body, 0)
        other = pl.ds(pl.multiple_of((1 - core) * T, T), T)
        for what in range(2):
            sbs[s, what] = kacc[s, what, other, :].astype(BF16)
        send(sib_send(s))

    mine = pl.ds(pl.multiple_of(core * T, T), T)

    def own_part(s, what):
        return kacc[s, what, mine, :] + sbr[s, what].astype(F32)

    x_target = [x_right, x_left, x_left, x_left, x_right, x_right]

    def x_sum(i):
        return copy(xs.at[i], xr.at[i], xr_s.at[i], xr_r.at[i], x_target[i])

    key_part(2, 2, 0, jnp.where(x >= 2, Z, 0))
    key_part(1, 1, 0, jnp.where(x >= 1, Z, 0))
    z_add(2)
    sib_send(2).wait_recv()
    for what in range(2):
        xs[what] = own_part(2, what).astype(BF16)
        send(x_sum(what))
    key_part(3, 0, 4, jnp.where(x == X - 1, z + 1, 4))
    key_part(0, 0, z + 1, Z + 1)
    z_add(3)
    sib_send(1).wait_recv()
    xs[2] = own_part(1, 0).astype(BF16)
    send(x_sum(2))
    x_sum(1).wait_recv()
    xs[3] = (own_part(1, 1) + xr[1].astype(F32)).astype(BF16)
    send(x_sum(3))
    sib_send(3).wait_recv()
    xs[5] = own_part(3, 1).astype(BF16)
    send(x_sum(5))
    x_sum(0).wait_recv()
    xs[4] = (own_part(3, 0) + xr[0].astype(F32)).astype(BF16)
    send(x_sum(4))

    sib_send(0).wait_recv()
    for i in (2, 5, 3, 4):
        x_sum(i).wait_recv()
    dk_ref[...] = (own_part(0, 0) + xr[2].astype(F32) + xr[4].astype(F32)).astype(BF16)
    dv_ref[...] = (own_part(0, 1) + xr[3].astype(F32) + xr[5].astype(F32)).astype(BF16)

    for what, out in ((0, att_ref), (1, dq_ref)):
        part = acc[0, what]
        for d in range(2):
            z_sum(d, 3, what).wait_recv()
            part = part + zr[d, 3, what].astype(F32)
        out[...] = part.T.astype(BF16)

    for op in started:
        op.wait_send()
    for ops in (q_right[1:], q_left[1:], g_right[1:], g_left[1:]):
        for op in ops:
            op.wait_send()
    for r in range(1, Z):
        stat_send(r).wait_send()
    for d in range(2):
        z_sum(d, 0, d).wait_send()


def per_device(queries, keys, values, out_grad, segments):
    seg = segments.astype(BF16).reshape(T // HD, HD)
    seg = jnp.pad(seg, ((0, SEG_ROWS - T // HD), (0, 0)))
    tile = jax.ShapeDtypeStruct((T, HD), BF16)
    vmem = pl.BlockSpec(memory_space=pltpu.VMEM)
    dma = pltpu.SemaphoreType.DMA
    return pl.pallas_call(
        kernel,
        out_shape=(tile,) * 4,
        in_specs=[vmem] * 5,
        out_specs=(vmem,) * 4,
        scratch_shapes=[
            pltpu.VMEM((Z, T + SEG_ROWS, HD), BF16),
            pltpu.VMEM((Z, T, HD), BF16),
            pltpu.VMEM((X, 2, T + SEG_ROWS, HD), BF16),
            pltpu.VMEM((X, 2, T, HD), BF16),
            pltpu.VMEM((X, HD, C), BF16),
            pltpu.VMEM((X, HD, C), BF16),
            pltpu.VMEM((Z, 3, C, T), F32),
            pltpu.VMEM((Z, 3, C, T), F32),
            pltpu.VMEM((3, C, Z * T), BF16),
            pltpu.VMEM((3, C, Z * T), BF16),
            pltpu.VMEM((Z, 2, HD, T), F32),
            pltpu.VMEM((X, 2, C, HD), F32),
            pltpu.VMEM((X, 16, T), F32),
            pltpu.VMEM((Z, 8, T), F32),
            pltpu.VMEM((Z, 8, T), F32),
            pltpu.VMEM((Z, 8, T), F32),
            pltpu.VMEM((2, 4, 2, HD, T), BF16),
            pltpu.VMEM((2, 4, 2, HD, T), BF16),
            pltpu.VMEM((X, 2, T, HD), BF16),
            pltpu.VMEM((X, 2, T, HD), BF16),
            pltpu.VMEM((6, T, HD), BF16),
            pltpu.VMEM((6, T, HD), BF16),
            dma((Z,)), dma((Z,)), dma((Z,)), dma((Z,)),
            dma((14,)), dma((14,)),
            dma((Z,)), dma((Z,)), dma((Z,)), dma((Z,)),
            dma((2, 4, 2)), dma((2, 4, 2)),
            dma((X,)), dma((X,)), dma((6,)), dma((6,)),
        ],
        compiler_params=pltpu.CompilerParams(
            collective_id=0, has_side_effects=True, vmem_limit_bytes=58 * 1024 * 1024
        ),
        cost_estimate=pl.CostEstimate(
            flops=4 * 10**9, bytes_accessed=600_000, transcendentals=2 * 10**6
        ),
    )(queries, keys, values, out_grad, seg)


def solution(mesh):
    rows = P(("dp", "ctx"), None)
    return jax.shard_map(
        per_device,
        mesh=mesh,
        in_specs=(rows, rows, rows, rows, P(("dp", "ctx"))),
        out_specs=(rows, rows, rows, rows),
        check_vma=False,
    )
```

time: 366 us -> 71.7 us (0.20)
  waiting for transfers between devices: 123 us -> 0 us
  blocking collectives: 107 us -> 0 us
  matrix products: 74.6 us -> 0 us
  Pallas kernels: 0 us -> 65.6 us
  starting transfers between devices: 28.6 us -> 0 us
  between operations: 13.9 us -> 0.65 us
  other arithmetic: 10.3 us -> 0.68 us
    all_gather x4 -> x0, waiting for transfers between devices: 90.3 us -> none  [the longest x1 60.3 us: per_device(): value_piece = lax.all_gather(values, 'ctx', axis=0, tiled=True)]
    all_gather x2 -> x0, blocking collectives: 84.3 us -> none  [the longest x1 42.3 us: per_device(): lax.all_gather(log_total, 'ctx', axis=0, tiled=True)]
    dot_general x6 -> x0, matrix products: 74.6 us -> none  [the longest x1 17.1 us: per_device(): jnp.dot(score_grad, key_piece, preferred_element_type=jnp.float32)]
    pallas_call x0 -> x1, Pallas kernels: none -> 65.6 us  [per_device(): pl.pallas_call(kernel, out_shape=(tile,) * 4, in_specs=[vmem] * 5, out_sp...]
    ppermute x12 -> x0, waiting for transfers between devices: 31.2 us -> none  [swapped(): return lax.ppermute(block, axis, route)]
    ppermute x12 -> x0, starting transfers between devices: 28.4 us -> none  [swapped(): return lax.ppermute(block, axis, route)]
    psum x1 -> x0, blocking collectives: 22.2 us -> none  [per_device(): counts = lax.psum(jnp.sum(one_hot, axis=0), 'ctx')]
    reduce_sum x3 -> x0, other arithmetic: 7.53 us -> none  [the longest x1 5.97 us: per_device(): totals = jnp.sum(exps, axis=1)]
  transfers between devices with their start and end apart: 16 -> 0, of which waited for: 14 -> 0; matrix products, arithmetic and copies ran while one was open for 17% -> 0% of each run, Pallas kernels for 0% -> 0%
where the time goes in v1:
time: 71.7 us; the launch traced here: 71.4 us
  Pallas kernels  65.6 us (91%)
  local copies, waits for them, and re-layouts  4.46 us (6%)
    pallas_call x1, Pallas kernels, per_device(): pl.pallas_call(kernel, out_shape=(tile,) * 4, in_specs=[vmem] * 5, out_sp...  65.6 us
    unnamed x10, local copies, waits for them, and re-layouts  3.86 us

profile of v1, /device:TPU:8, one launch (start us, length us, event | category | flops | bytes accessed | tf_op | source)
XLA Modules:
  0.0 71.4 jit_solution(2734339187921951664)
XLA Ops:
  0.6 0.7 convert_bitcast_fusion
  1.3 0.6 pad.4.seg_ref
  1.9 65.6 %shard_map.84 = (bf16[256,128]{1,0:T(8,128)(2,1)}, bf16[256,128]{1,0:T(8,128)(2,1)}, bf16[256,128]{1,0:T(8,128)(2,1)}, bf16[256,128]{1,0:T(8,128)(2,1)}) custom-call(bf16[256,128]{1,0:T(8,128)(2,1)} %q_ref.1, bf16[256,128]{1,0:T(8,128)(2,1)} %k_ref.1, bf16[256,128]{1,0:T(8,128)(2,1)} %v_ref.1, bf16[256,128]{1,0:T(8,128)(2,1)} %g_ref.1, ...), custom_call_target="tpu_custom_call" | custom-call | flops 4000000000 | bytes 600000 | tf_op jit(solution)/shard_map/pallas_call | solution.py:373
  67.5 0.0 copy-start.2
  67.5 1.5 %copy.13 = bf16[256,128]{1,0:T(8,128)(2,1)} copy(bf16[256,128]{1,0:T(8,128)(2,1)} %get-tuple-element.8) | data formatting | bytes 131072
  69.0 0.0 copy-done.2
  69.0 0.0 copy-start.1
  69.0 0.6 copy.14
  69.7 0.2 copy-done.1
  69.9 0.0 copy-start
  69.9 0.6 copy.15
  70.5 0.2 copy-done
  70.8 0.6 copy.16
Async XLA Ops:
  67.5 1.5 %copy-start.2 = (bf16[256,128]{1,0:T(8,128)(2,1)S(1)}, bf16[256,128]{1,0:T(8,128)(2,1)}, u32[]{:S(2)}) copy-start(bf16[256,128]{1,0:T(8,128)(2,1)} %get-tuple-element.9) | copy-start | bytes 196612
  69.0 0.9 %copy-start.1 = (bf16[256,128]{1,0:T(8,128)(2,1)S(1)}, bf16[256,128]{1,0:T(8,128)(2,1)}, u32[]{:S(2)}) copy-start(bf16[256,128]{1,0:T(8,128)(2,1)} %get-tuple-element.10) | copy-start | bytes 196612
  69.9 0.9 %copy-start = (bf16[256,128]{1,0:T(8,128)(2,1)S(1)}, bf16[256,128]{1,0:T(8,128)(2,1)}, u32[]{:S(2)}) copy-start(bf16[256,128]{1,0:T(8,128)(2,1)} %get-tuple-element.11) | copy-start | bytes 196612

commit v2 on v1

v2 whole, which is shorter than its diff:
```python
import functools
import math

import jax
import jax.numpy as jnp
from jax import lax
from jax.experimental import pallas as pl
from jax.experimental.pallas import tpu as pltpu
from jax.sharding import PartitionSpec as P

MESH = pl.DeviceIdType.MESH
HD = 128
X, Z = 4, 8
T = 256
C = 2 * T
SEG_ROWS = 16
NEG = -1e30
INV_ROOT = 1.0 / math.sqrt(HD)
ALPHA = INV_ROOT * math.log2(math.e)
F32 = jnp.float32
BF16 = jnp.bfloat16
NT = (((1,), (1,)), ((), ()))


def dot_nt(a, b):
    return lax.dot_general(a, b, NT, preferred_element_type=F32)


def dot(a, b):
    return jnp.dot(a, b, preferred_element_type=F32)


def pick(index, values):
    result = values[-1]
    for i in range(len(values) - 2, -1, -1):
        result = jnp.where(index == i, values[i], result)
    return result


def kernel(
    q_ref, k_ref, v_ref, g_ref, seg_ref, out_ref,
    segf, qs, gs, qt, gt, ks, vs, vkt, eb, tb, pst, run, accv, accw, kacc, cnt,
    str_, fin, zs, zr, sbs, sbr, xs, xr,
    zq_s, zq_r, zg_s, zg_r, kv_s, kv_r, st_s, st_r, fn_s, fn_r,
    za_s, za_r, sb_s, sb_r, xr_s, xr_r,
):
    ctx = lax.axis_index("ctx")
    x = ctx // (2 * Z)
    z = (ctx // 2) % Z
    core = ctx % 2

    def dev(xx, zz, cc):
        return {"ctx": ((xx + X) % X) * (2 * Z) + ((zz + Z) % Z) * 2 + cc}

    sib = dev(x, z, 1 - core)
    z_right, z_left = dev(x, z + 1, core), dev(x, z - 1, core)
    x_right, x_left = dev(x + 1, z, core), dev(x - 1, z, core)

    barrier = pltpu.get_barrier_semaphore()
    for peer in (z_right, z_left, x_right, x_left, sib):
        pl.semaphore_signal(barrier, inc=1, device_id=peer, device_id_type=MESH)

    segf[...] = jnp.zeros_like(segf)
    segf[0 : T // HD, :] = seg_ref[...].astype(F32)
    seg_rows = segf[...].astype(BF16)
    qs[0, 0:T, :] = q_ref[...]
    qs[0, T : T + SEG_ROWS, :] = seg_rows
    gs[0] = g_ref[...]
    ks[0, core, 0:T, :] = k_ref[...]
    ks[0, core, T : T + SEG_ROWS, :] = seg_rows
    vs[0, core] = v_ref[...]

    pl.semaphore_wait(barrier, 5)

    started = []

    def copy(src, dst, send, recv, target):
        return pltpu.make_async_remote_copy(
            src_ref=src, dst_ref=dst, send_sem=send, recv_sem=recv,
            device_id=target, device_id_type=MESH,
        )

    def send(op):
        op.start()
        started.append(op)

    def q_hop(src, dst, target):
        return copy(qs.at[src], qs.at[dst], zq_s.at[dst], zq_r.at[dst], target)

    def g_hop(src, dst, target):
        return copy(gs.at[src], gs.at[dst], zg_s.at[dst], zg_r.at[dst], target)

    def k_hop(i, src, dst, target):
        return copy(ks.at[src, core], ks.at[dst, core], kv_s.at[i], kv_r.at[i], target)

    def v_hop(i, src, dst, target):
        return copy(vs.at[src, core], vs.at[dst, core], kv_s.at[i], kv_r.at[i], target)

    q_right = [q_hop(j, j + 1, z_right) for j in range(4)]
    q_left = [q_hop((8 - j) % 8, 7 - j, z_left) for j in range(3)]
    g_right = [g_hop(j, j + 1, z_right) for j in range(3)]
    g_left = [g_hop((8 - j) % 8, 7 - j, z_left) for j in range(4)]
    k_sib = [k_hop(s, s, s, sib) for s in range(4)]
    v_sib = [v_hop(4 + s, s, s, sib) for s in range(4)]
    k_right, v_right = k_hop(8, 0, 1, x_right), v_hop(9, 0, 1, x_right)
    k_left, v_left = k_hop(10, 0, 3, x_left), v_hop(11, 0, 3, x_left)
    k_far, v_far = k_hop(12, 1, 2, x_right), v_hop(13, 3, 2, x_left)

    for op in (
        q_right[0], q_left[0], k_sib[0], v_sib[0], k_right, k_left,
        g_right[0], g_left[0], v_right, v_left,
    ):
        op.start()

    def z_step(j):
        q_right[j - 1].wait_recv()
        if j < 4:
            q_right[j].start()
            q_left[j - 1].wait_recv()
        if j < 3:
            q_left[j].start()
        g_left[j - 1].wait_recv()
        if j < 4:
            g_left[j].start()
            g_right[j - 1].wait_recv()
        if j < 3:
            g_right[j].start()

    doc16 = lax.broadcasted_iota(jnp.int32, (16, HD), 0).astype(F32)

    def prepare_keys(s):
        below = jnp.zeros((16, HD), F32)
        for c in range(2):
            vkt[s, 0:HD, c * T : (c + 1) * T] = vs[s, c].T
            vkt[s, HD:, c * T : (c + 1) * T] = ks[s, c, 0:T, :].T
            seg = ks[s, c, T : T + SEG_ROWS, :].astype(F32)
            for h in range(T // HD):
                below += jnp.where(seg[h : h + 1, :] < doc16, 1.0, 0.0)
        cnt[s] = jnp.broadcast_to(jnp.sum(below, axis=1, keepdims=True), (16, T))

    def prepare_queries(r):
        qt[r] = qs[r, 0:T, :].T
        gt[r] = gs[r].T

    key_row = lax.broadcasted_iota(jnp.int32, (T, T), 0).astype(F32)
    query_lane = lax.broadcasted_iota(jnp.int32, (1, T), 1).astype(F32)
    doc_q = lax.broadcasted_iota(jnp.int32, (16, T), 0).astype(F32)

    def slots(r):
        own = (r == 0) | (r > z)
        used = own | ((x == X - 1) & (r >= 4))
        return jnp.where(used, 0, 1), jnp.where(own, 0, 3), jnp.minimum(x, 2) + 1

    def piece(r, u, s):
        seg = qs[r, T : T + SEG_ROWS, :].astype(F32)
        seg_q = jnp.concatenate([seg[0:1, :], seg[1:2, :]], axis=1)
        low = jnp.sum(jnp.where(seg_q == doc_q, cnt[s], 0.0), axis=0, keepdims=True)
        diagonal = (s == 0) & (r == 0)
        high = jnp.where(diagonal, query_lane + (core * T).astype(F32), 1e9)
        q = qs[r, 0:T, :]
        g = gs[r]
        scores = []
        for c in range(2):
            sc = dot_nt(ks[s, c, 0:T, :], q)
            pos = key_row + c * T
            scores.append(jnp.where((pos >= low) & (pos <= high), sc, NEG))
        top = jnp.max(jnp.maximum(scores[0], scores[1]), axis=0, keepdims=True)
        exps = [jnp.exp2((sc - top) * ALPHA) for sc in scores]
        grads = [dot_nt(vs[s, c], g) for c in range(2)]
        total = jnp.sum(exps[0] + exps[1], axis=0, keepdims=True)
        moment = jnp.sum(exps[0] * grads[0] + exps[1] * grads[1], axis=0, keepdims=True)
        mean = moment / total
        for c in range(2):
            rows = slice(c * T, (c + 1) * T)
            eb[r, u, rows, :] = exps[c].astype(BF16)
            tb[r, u, rows, :] = (exps[c] * (grads[c] - mean)).astype(BF16)
        part_v = dot(vkt[s], eb[r, u])
        part_t = dot(vkt[s, HD:, :], tb[r, u])
        pst[r, u, 0:1, :] = top
        pst[r, u, 1:2, :] = mean
        old = run[r, 0:1, :]
        new = jnp.maximum(old, top)
        keep = jnp.exp2((old - new) * ALPHA)
        add = jnp.exp2((top - new) * ALPHA)
        run[r, 0:1, :] = new
        run[r, 1:2, :] = run[r, 1:2, :] * keep + total * add
        run[r, 2:3, :] = run[r, 2:3, :] * keep + moment * add
        accv[r] = accv[r] * keep + part_v * add
        accw[r] = accw[r] * keep + (part_t + mean * part_v[HD:, :]) * add

    def stat_send(r):
        return copy(run.at[r], str_.at[r], st_s.at[r], st_r.at[r], dev(x, z - r, core))

    def clear(r, _):
        run[r, 0:1, :] = jnp.full((1, T), NEG, F32)
        run[r, 1:8, :] = jnp.zeros((7, T), F32)
        accv[r] = jnp.zeros((2 * HD, T), F32)
        accw[r] = jnp.zeros((HD, T), F32)
        return 0

    lax.fori_loop(0, Z, clear, 0)

    def wave(w, _):
        @pl.when(w == 0)
        def _():
            prepare_queries(0)
            k_sib[0].wait_recv()
            v_sib[0].wait_recv()
            prepare_keys(0)

        @pl.when(w == 1)
        def _():
            q_right[0].wait_recv()
            q_right[1].start()
            q_left[0].wait_recv()
            q_left[1].start()
            k_right.wait_recv()
            k_far.start()
            k_sib[1].start()
            k_left.wait_recv()
            k_sib[3].start()
            g_left[0].wait_recv()
            g_left[1].start()
            g_right[0].wait_recv()
            g_right[1].start()
            v_left.wait_recv()
            v_far.start()
            v_sib[3].start()
            v_right.wait_recv()
            v_sib[1].start()
            prepare_queries(1)
            prepare_queries(7)
            k_sib[1].wait_recv()
            v_sib[1].wait_recv()
            prepare_keys(1)
            k_sib[3].wait_recv()
            v_sib[3].wait_recv()
            prepare_keys(3)

        @pl.when(w == 2)
        def _():
            z_step(2)
            k_far.wait_recv()
            k_sib[2].start()
            v_far.wait_recv()
            v_sib[2].start()
            prepare_queries(2)
            prepare_queries(6)

        @pl.when(w == 3)
        def _():
            k_sib[2].wait_recv()
            v_sib[2].wait_recv()
            prepare_keys(2)

        @pl.when(w == 4)
        def _():
            z_step(3)
            prepare_queries(3)
            prepare_queries(5)

        @pl.when(w == 5)
        def _():
            z_step(4)
            prepare_queries(4)

        i_low, i_high = pick(w, [0, 0, 3, 0, 5, 7]), pick(w, [1, 3, 5, 5, 7, 8])
        u_from, u_to = pick(w, [0, 0, 0, 2, 0, 0]), pick(w, [1, 2, 2, 3, 3, 3])

        def block(i, _):
            r = jnp.where(i % 2 == 1, (i + 1) // 2, (8 - i // 2) % 8)
            u_low, s_zero, u_high = slots(r)
            u_first = jnp.where((w == 1) & (i == 0), 1, u_from)

            def body(u, _):
                piece(r, u, jnp.where(u == 0, s_zero, u))
                return 0

            lax.fori_loop(jnp.maximum(u_low, u_first), jnp.minimum(u_high, u_to), body, 0)

            @pl.when((w >= 3) & (r > 0))
            def _():
                stat_send(r).start()

            return 0

        lax.fori_loop(i_low, i_high, block, 0)
        return 0

    lax.fori_loop(0, 6, wave, 0)

    for r in (1, 7, 2, 6, 3, 5, 4):
        stat_send(r).wait_recv()
    tops = [run[0, 0:1, :]] + [str_[r, 0:1, :] for r in range(1, Z)]
    top = functools.reduce(jnp.maximum, tops)
    total = jnp.zeros((1, T), F32)
    moment = jnp.zeros((1, T), F32)
    for r in range(Z):
        box = run if r == 0 else str_
        scale = jnp.exp2((tops[r] - top) * ALPHA)
        total += box[r, 1:2, :] * scale
        moment += box[r, 2:3, :] * scale
    inverse = 1.0 / total
    fin[0, 0:1, :] = top
    fin[0, 1:2, :] = inverse
    fin[0, 2:3, :] = moment * inverse

    def fin_send(r):
        return copy(fin.at[0], fin.at[r], fn_s.at[r], fn_r.at[r], dev(x, z + r, core))

    for r in (4, 3, 5, 2, 6, 1, 7):
        send(fin_send(r))

    def z_sum(d, i, what):
        return copy(
            zs.at[d, i, what], zr.at[d, i, what], za_s.at[d, i, what], za_r.at[d, i, what],
            z_right if d == 0 else z_left,
        )

    def z_part(r, what):
        scale = jnp.exp2((run[r, 0:1, :] - fin[r, 0:1, :]) * ALPHA) * fin[r, 1:2, :]
        if what == 0:
            return accv[r, 0:HD, :] * scale
        return (accw[r] - fin[r, 2:3, :] * accv[r, HD:, :]) * (scale * INV_ROOT)

    def z_add(i):
        for what in range(2):
            for d in range(2):
                r = 4 + i if d == 0 else 4 - i
                if i == 0 and what != d:
                    continue
                part = z_part(r, what)
                if i > 1 or (i == 1 and what == d):
                    z_sum(d, i - 1, what).wait_recv()
                    part = part + zr[d, i - 1, what].astype(F32)
                zs[d, i, what] = part.astype(BF16)
                send(z_sum(d, i, what))

    def sib_send(s):
        return copy(sbs.at[s], sbr.at[s], sb_s.at[s], sb_r.at[s], sib)

    mine = pl.ds(pl.multiple_of(core * T, T), T)
    other = pl.ds(pl.multiple_of((1 - core) * T, T), T)

    def key_part(s, u, r_low, r_high):
        kacc[s] = jnp.zeros((2 * HD, C), F32)

        def body(i, _):
            r = i % Z
            scale = jnp.exp2((pst[r, u, 0:1, :] - fin[r, 0:1, :]) * ALPHA) * fin[r, 1:2, :]
            root = scale * INV_ROOT
            shift = root * (pst[r, u, 1:2, :] - fin[r, 2:3, :])
            q = qt[r].astype(F32)
            left = jnp.concatenate(
                [(gt[r].astype(F32) * scale).astype(BF16), (q * shift).astype(BF16)], axis=0
            )
            sum_e = dot_nt(left, eb[r, u])
            sum_t = dot_nt((q * root).astype(BF16), tb[r, u])
            kacc[s, 0:HD, :] += sum_e[0:HD, :]
            kacc[s, HD:, :] += sum_e[HD:, :] + sum_t
            return 0

        lax.fori_loop(r_low, r_high, body, 0)
        sbs[s] = kacc[s, :, other].astype(BF16)
        send(sib_send(s))

    def own_part(s, what):
        rows = slice(what * HD, (what + 1) * HD)
        return kacc[s, rows, mine] + sbr[s, rows, :].astype(F32)

    x_target = [x_right, x_left, x_left, x_left, x_right, x_right]

    def x_sum(i):
        return copy(xs.at[i], xr.at[i], xr_s.at[i], xr_r.at[i], x_target[i])

    def x_send(i, part):
        xs[i] = part.astype(BF16)
        send(x_sum(i))

    for r in (4, 5, 3, 6, 2, 7, 1):
        fin_send(r).wait_recv()
        if r == 4:
            z_add(0)
    key_part(2, 2, 0, jnp.where(x >= 2, Z, 0))
    z_add(1)
    sib_send(2).wait_recv()
    x_send(0, own_part(2, 0))
    x_send(1, own_part(2, 1))
    key_part(1, 1, 0, jnp.where(x >= 1, Z, 0))
    z_add(2)
    sib_send(1).wait_recv()
    x_send(2, own_part(1, 0))
    key_part(3, 0, 4, jnp.where(x == X - 1, z + 1, 4))
    sib_send(3).wait_recv()
    x_send(5, own_part(3, 1))
    x_sum(1).wait_recv()
    x_send(3, own_part(1, 1) + xr[1].astype(F32))
    x_sum(0).wait_recv()
    x_send(4, own_part(3, 0) + xr[0].astype(F32))
    key_part(0, 0, z + 1, Z + 1)
    z_add(3)
    sib_send(0).wait_recv()
    for what, near in ((0, (2, 4)), (1, (3, 5))):
        part = own_part(0, what)
        for i in near:
            x_sum(i).wait_recv()
            part = part + xr[i].astype(F32)
        out_ref[3 - what] = part.T.astype(BF16)

    for what in range(2):
        part = z_part(0, what)
        for d in range(2):
            z_sum(d, 3, what).wait_recv()
            part = part + zr[d, 3, what].astype(F32)
        out_ref[what] = part.T.astype(BF16)

    for op in (*q_right, *q_left, *g_right, *g_left, *k_sib, *v_sib):
        op.wait_send()
    for op in (k_right, v_right, k_left, v_left, k_far, v_far, *started):
        op.wait_send()
    for r in range(1, Z):
        stat_send(r).wait_send()


def hand_on(all_ref, *outs):
    for i, out in enumerate(outs):
        out[...] = all_ref[i]


def per_device(queries, keys, values, out_grad, segments):
    vmem = pl.BlockSpec(memory_space=pltpu.VMEM)
    dma = pltpu.SemaphoreType.DMA
    sums = pl.pallas_call(
        kernel,
        out_shape=jax.ShapeDtypeStruct((4, T, HD), BF16),
        in_specs=[vmem] * 5,
        out_specs=vmem,
        scratch_shapes=[
            pltpu.VMEM((SEG_ROWS, HD), F32),
            pltpu.VMEM((Z, T + SEG_ROWS, HD), BF16),
            pltpu.VMEM((Z, T, HD), BF16),
            pltpu.VMEM((Z, HD, T), BF16),
            pltpu.VMEM((Z, HD, T), BF16),
            pltpu.VMEM((X, 2, T + SEG_ROWS, HD), BF16),
            pltpu.VMEM((X, 2, T, HD), BF16),
            pltpu.VMEM((X, 2 * HD, C), BF16),
            pltpu.VMEM((Z, 3, C, T), BF16),
            pltpu.VMEM((Z, 3, C, T), BF16),
            pltpu.VMEM((Z, 3, 8, T), F32),
            pltpu.VMEM((Z, 8, T), F32),
            pltpu.VMEM((Z, 2 * HD, T), F32),
            pltpu.VMEM((Z, HD, T), F32),
            pltpu.VMEM((X, 2 * HD, C), F32),
            pltpu.VMEM((X, 16, T), F32),
            pltpu.VMEM((Z, 8, T), F32),
            pltpu.VMEM((Z, 8, T), F32),
            pltpu.VMEM((2, 4, 2, HD, T), BF16),
            pltpu.VMEM((2, 4, 2, HD, T), BF16),
            pltpu.VMEM((X, 2 * HD, T), BF16),
            pltpu.VMEM((X, 2 * HD, T), BF16),
            pltpu.VMEM((6, HD, T), BF16),
            pltpu.VMEM((6, HD, T), BF16),
            dma((Z,)), dma((Z,)), dma((Z,)), dma((Z,)),
            dma((14,)), dma((14,)),
            dma((Z,)), dma((Z,)), dma((Z,)), dma((Z,)),
            dma((2, 4, 2)), dma((2, 4, 2)),
            dma((X,)), dma((X,)), dma((6,)), dma((6,)),
        ],
        compiler_params=pltpu.CompilerParams(
            collective_id=0, has_side_effects=True, vmem_limit_bytes=58 * 1024 * 1024
        ),
        cost_estimate=pl.CostEstimate(
            flops=4 * 10**9, bytes_accessed=600_000, transcendentals=2 * 10**6
        ),
    )(queries, keys, values, out_grad, segments.reshape(T // HD, HD))
    return pl.pallas_call(
        hand_on,
        out_shape=(jax.ShapeDtypeStruct((T, HD), BF16),) * 4,
        in_specs=[vmem],
        out_specs=(vmem,) * 4,
    )(sums)


def solution(mesh):
    rows = P(("dp", "ctx"), None)
    return jax.shard_map(
        per_device,
        mesh=mesh,
        in_specs=(rows, rows, rows, rows, P(("dp", "ctx"))),
        out_specs=(rows, rows, rows, rows),
        check_vma=False,
    )
```

time: 71.7 us -> 61 us (0.85)
  the two profiles are of different devices: /device:TPU:8 before, /device:TPU:1 now
where the time goes in v2:
time: 61 us; the launch traced here: 60.9 us
  Pallas kernels  60.2 us (99%)
  between operations  0.64 us (1%)
    pallas_call x1, Pallas kernels, per_device(): pl.pallas_call(kernel, out_shape=jax.ShapeDtypeStruct((4, T, HD), BF16),...  58.6 us
    pallas_call x1, Pallas kernels, per_device(): pl.pallas_call(hand_on, out_shape=(jax.ShapeDtypeStruct((T, HD), BF16),)...  1.65 us

profile of v2, /device:TPU:1, one launch (start us, length us, event | category | flops | bytes accessed | tf_op | source)
XLA Modules:
  0.0 60.9 jit_solution(147031451927859221)
XLA Ops:
  0.6 58.6 %shard_map.84.all_ref = bf16[4,256,128]{2,1,0:T(8,128)(2,1)} custom-call(bf16[256,128]{1,0:T(8,128)(2,1)} %q_ref.1, bf16[256,128]{1,0:T(8,128)(2,1)} %k_ref.1, bf16[256,128]{1,0:T(8,128)(2,1)} %v_ref.1, bf16[256,128]{1,0:T(8,128)(2,1)} %g_ref.1, s32[2,128]{1,0:T(2,128)} %bitcast.1), custom_call_target="tpu_custom_call" | custom-call | flops 4000000000 | bytes 600000 | tf_op jit(solution)/shard_map/pallas_call | solution.py:433
  59.2 1.7 %shard_map.85 = (bf16[256,128]{1,0:T(8,128)(2,1)}, bf16[256,128]{1,0:T(8,128)(2,1)}, bf16[256,128]{1,0:T(8,128)(2,1)}, bf16[256,128]{1,0:T(8,128)(2,1)}) custom-call(bf16[4,256,128]{2,1,0:T(8,128)(2,1)} %shard_map.84.all_ref), custom_call_target="tpu_custom_call" | custom-call | tf_op jit(solution)/shard_map/pallas_call | solution.py:476

commit v3 on v2

v3 whole, which is shorter than its diff:
```python
import functools
import math

import jax
import jax.numpy as jnp
from jax import lax
from jax.experimental import pallas as pl
from jax.experimental.pallas import tpu as pltpu
from jax.sharding import PartitionSpec as P

MESH = pl.DeviceIdType.MESH
HD = 128
X, Z = 4, 8
T = 256
C = 2 * T
SEG_ROWS = 16
NEG = -1e30
INV_ROOT = 1.0 / math.sqrt(HD)
ALPHA = INV_ROOT * math.log2(math.e)
F32 = jnp.float32
BF16 = jnp.bfloat16
NT = (((1,), (1,)), ((), ()))


def dot_nt(a, b):
    return lax.dot_general(a, b, NT, preferred_element_type=F32)


def dot(a, b):
    return jnp.dot(a, b, preferred_element_type=F32)


def kernel(
    q_ref, k_ref, v_ref, g_ref, seg_ref, out_ref,
    segf, qs, gs, qt, gt, ks, vs, vkt, eb, tb, sbuf, dbuf, pst, run, accv, accw,
    left_e, left_t, kacc, cnt, sto, sti, fin, zs, zr, sbs, sbr, xs, xr,
    zq_s, zq_r, zg_s, zg_r, kv_s, kv_r, st_s, st_r, fn_s, fn_r,
    za_s, za_r, sb_s, sb_r, xr_s, xr_r,
):
    ctx = lax.axis_index("ctx")
    x = ctx // (2 * Z)
    z = (ctx // 2) % Z
    core = ctx % 2

    def dev(xx, zz, cc):
        return {"ctx": ((xx + X) % X) * (2 * Z) + ((zz + Z) % Z) * 2 + cc}

    sib = dev(x, z, 1 - core)
    z_right, z_left = dev(x, z + 1, core), dev(x, z - 1, core)
    x_right, x_left = dev(x + 1, z, core), dev(x - 1, z, core)

    barrier = pltpu.get_barrier_semaphore()
    for peer in (z_right, z_left, x_right, x_left, sib):
        pl.semaphore_signal(barrier, inc=1, device_id=peer, device_id_type=MESH)

    segf[...] = jnp.zeros_like(segf)
    segf[0 : T // HD, :] = seg_ref[...].astype(F32)
    seg_rows = segf[...].astype(BF16)
    qs[0, 0:T, :] = q_ref[...]
    qs[0, T : T + SEG_ROWS, :] = seg_rows
    gs[0] = g_ref[...]
    ks[0, core, 0:T, :] = k_ref[...]
    ks[0, core, T : T + SEG_ROWS, :] = seg_rows
    vs[0, core] = v_ref[...]

    pl.semaphore_wait(barrier, 5)

    def copy(src, dst, send, recv, target):
        return pltpu.make_async_remote_copy(
            src_ref=src, dst_ref=dst, send_sem=send, recv_sem=recv,
            device_id=target, device_id_type=MESH,
        )

    started = []

    def send(op):
        op.start()
        started.append(op)

    half = (slice(0, HD), slice(HD, T + SEG_ROWS))

    def q_hop(src, dst, target, h):
        return copy(
            qs.at[src, half[h], :], qs.at[dst, half[h], :], zq_s.at[dst, h], zq_r.at[dst, h], target
        )

    def g_hop(src, dst, target, h):
        rows = slice(h * HD, (h + 1) * HD)
        return copy(gs.at[src, rows, :], gs.at[dst, rows, :], zg_s.at[dst, h], zg_r.at[dst, h], target)

    def k_hop(i, src, dst, target):
        return copy(ks.at[src, core], ks.at[dst, core], kv_s.at[i], kv_r.at[i], target)

    def v_hop(i, src, dst, target):
        return copy(vs.at[src, core], vs.at[dst, core], kv_s.at[i], kv_r.at[i], target)

    q_right = [[q_hop(j, j + 1, z_right, h) for h in range(2)] for j in range(4)]
    q_left = [[q_hop((8 - j) % 8, 7 - j, z_left, h) for h in range(2)] for j in range(3)]
    g_right = [[g_hop(j, j + 1, z_right, h) for h in range(2)] for j in range(3)]
    g_left = [[g_hop((8 - j) % 8, 7 - j, z_left, h) for h in range(2)] for j in range(4)]
    k_sib = [k_hop(s, s, s, sib) for s in range(4)]
    v_sib = [v_hop(4 + s, s, s, sib) for s in range(4)]
    k_right, v_right = k_hop(8, 0, 1, x_right), v_hop(9, 0, 1, x_right)
    k_left, v_left = k_hop(10, 0, 3, x_left), v_hop(11, 0, 3, x_left)
    k_far, v_far = k_hop(12, 1, 2, x_right), v_hop(13, 3, 2, x_left)

    for op in (
        q_right[0][0], q_left[0][0], k_right, k_left, k_sib[0], v_sib[0],
        q_right[0][1], q_left[0][1], v_left, v_right,
        g_right[0][0], g_left[0][0], g_right[0][1], g_left[0][1],
    ):
        op.start()

    def z_step(j):
        for right, left in ((q_right, q_left), (g_right, g_left)):
            for h in range(2):
                for hops in (right, left):
                    if j <= len(hops):
                        hops[j - 1][h].wait_recv()
                    if j < len(hops):
                        hops[j][h].start()

    doc16 = lax.broadcasted_iota(jnp.int32, (16, HD), 0).astype(F32)

    def prepare_keys(s):
        below = jnp.zeros((16, HD), F32)
        for c in range(2):
            lanes = slice(s * C + c * T, s * C + (c + 1) * T)
            vkt[0:HD, lanes] = vs[s, c].T
            vkt[HD:, lanes] = ks[s, c, 0:T, :].T
            seg = ks[s, c, T : T + SEG_ROWS, :].astype(F32)
            for h in range(T // HD):
                below += jnp.where(seg[h : h + 1, :] < doc16, 1.0, 0.0)
        cnt[s] = jnp.broadcast_to(jnp.sum(below, axis=1, keepdims=True), (16, T))

    def prepare_queries(r):
        qt[r] = qs[r, 0:T, :].T
        gt[r] = gs[r].T

    key_row = lax.broadcasted_iota(jnp.int32, (T, T), 0).astype(F32)
    query_lane = lax.broadcasted_iota(jnp.int32, (1, T), 1).astype(F32)
    doc_q = lax.broadcasted_iota(jnp.int32, (16, T), 0).astype(F32)

    def near_slot(r):
        own = (r == 0) | (r > z)
        used = own | ((x == X - 1) & (r >= 4))
        return used, jnp.where(own, 0, 3)

    def block_lanes(r):
        return pl.ds(pl.multiple_of(r * T, T), T)

    def piece(r, which, chunks, diagonal=False):
        seg = qs[r, T : T + SEG_ROWS, :].astype(F32)
        seg_q = jnp.concatenate([seg[0:1, :], seg[1:2, :]], axis=1)
        same = seg_q == doc_q
        q = qs[r, 0:T, :]
        g = gs[r]
        lanes = block_lanes(r)
        blocks = []
        top = jnp.full((1, T), NEG, F32)
        for u, s in chunks:
            low = jnp.sum(jnp.where(same, cnt[s], 0.0), axis=0, keepdims=True)
            if u == 2:
                low = jnp.where(x >= 2, low, 1e9)
            for c in range(2):
                b = len(blocks)
                sc = dot_nt(ks[s, c, 0:T, :], q)
                allowed = key_row >= low - c * T
                if diagonal:
                    allowed = allowed & (key_row <= query_lane + ((core - c) * T).astype(F32))
                sc = jnp.where(allowed, sc, NEG)
                sbuf[b] = sc
                top = jnp.maximum(top, jnp.max(sc, axis=0, keepdims=True))
                blocks.append((s, c, slice(u * C + c * T, u * C + (c + 1) * T)))
        total = jnp.zeros((1, T), F32)
        moment = jnp.zeros((1, T), F32)
        for b, (s, c, rows) in enumerate(blocks):
            e = jnp.exp2((sbuf[b] - top) * ALPHA)
            weighted = e * dot_nt(vs[s, c], g)
            eb[rows, lanes] = e.astype(BF16)
            sbuf[b] = e
            dbuf[b] = weighted
            total += jnp.sum(e, axis=0, keepdims=True)
            moment += jnp.sum(weighted, axis=0, keepdims=True)
        mean = moment / total
        for b, (s, c, rows) in enumerate(blocks):
            tb[rows, lanes] = (dbuf[b] - sbuf[b] * mean).astype(BF16)
        pst[r, which, 0:1, :] = top
        pst[r, which, 1:2, :] = mean
        old = run[r, 0:1, :]
        new = jnp.maximum(old, top)
        keep = jnp.exp2((old - new) * ALPHA)
        add = jnp.exp2((top - new) * ALPHA)
        run[r, 0:1, :] = new
        run[r, 1:2, :] = run[r, 1:2, :] * keep + total * add
        run[r, 2:3, :] = run[r, 2:3, :] * keep + moment * add

    def near_piece(r):
        used, s = near_slot(r)

        @pl.when(used)
        def _():
            piece(r, 0, [(0, s)])

    def products(r):
        lanes = block_lanes(r)

        def add_part(which, rows, keys):
            add = jnp.exp2((pst[r, which, 0:1, :] - run[r, 0:1, :]) * ALPHA)
            part_v = dot(vkt[:, keys], eb[rows, lanes])
            part_t = dot(vkt[HD:, keys], tb[rows, lanes])
            accv[r] += part_v * add
            accw[r] += (part_t + pst[r, which, 1:2, :] * part_v[HD:, :]) * add

        accv[r] = jnp.zeros((2 * HD, T), F32)
        accw[r] = jnp.zeros((HD, T), F32)
        used, s = near_slot(r)

        @pl.when(used)
        def _():
            add_part(0, slice(0, C), pl.ds(pl.multiple_of(s * C, C), C))

        @pl.when(x >= 1)
        def _():
            add_part(1, slice(C, 3 * C), slice(C, 3 * C))

    for r in range(Z):
        run[r, 0:1, :] = jnp.full((1, T), NEG, F32)
        run[r, 1:8, :] = jnp.zeros((7, T), F32)

    def pack(i, values):
        for n in range(3):
            for h in range(2):
                sto[i, 2 * n + h : 2 * n + h + 1, :] = values[n][:, h * HD : (h + 1) * HD]

    def merge(parts):
        top = functools.reduce(jnp.maximum, [p[0:2, :] for p in parts])
        scales = [jnp.exp2((p[0:2, :] - top) * ALPHA) for p in parts]
        total = sum(p[2:4, :] * scale for p, scale in zip(parts, scales))
        moment = sum(p[4:6, :] * scale for p, scale in zip(parts, scales))
        return top, total, moment

    def stat_send(r):
        return copy(sto.at[r], sti.at[32 + r], st_s.at[r], st_r.at[r], dev(x, z - r, core))

    far_blocks = (3, 5, 4)

    def total_send(kind, d):
        r = 0 if kind == 0 else far_blocks[kind - 1]
        slot = kind * Z + (d + r) % Z
        return copy(sto.at[r], sti.at[slot], fn_s.at[0], fn_r.at[0], dev(x, z + d, core))

    prepare_queries(0)
    k_sib[0].wait_recv()
    v_sib[0].wait_recv()
    prepare_keys(0)
    piece(0, 0, [(0, 0)], diagonal=True)

    k_right.wait_recv()
    k_far.start()
    k_sib[1].start()
    for h in range(2):
        q_right[0][h].wait_recv()
        q_right[1][h].start()
        q_left[0][h].wait_recv()
        q_left[1][h].start()
    k_left.wait_recv()
    k_sib[3].start()
    v_left.wait_recv()
    v_far.start()
    v_sib[3].start()
    v_right.wait_recv()
    v_sib[1].start()
    for h in range(2):
        g_right[0][h].wait_recv()
        g_right[1][h].start()
        g_left[0][h].wait_recv()
        g_left[1][h].start()
    prepare_queries(1)
    prepare_queries(7)
    for s in (1, 3):
        k_sib[s].wait_recv()
        v_sib[s].wait_recv()
        prepare_keys(s)
    k_far.wait_recv()
    k_sib[2].start()

    def early(i, _):
        near_piece(jnp.where(i == 0, 1, 7))
        return 0

    lax.fori_loop(0, 2, early, 0)
    z_step(2)
    v_far.wait_recv()
    v_sib[2].start()
    prepare_queries(2)
    prepare_queries(6)
    k_sib[2].wait_recv()
    v_sib[2].wait_recv()
    prepare_keys(2)

    def block(i, _):
        @pl.when(i == 3)
        def _():
            z_step(3)

        @pl.when(i == 5)
        def _():
            prepare_queries(3)
            prepare_queries(5)

        @pl.when(i == 7)
        def _():
            z_step(4)
            for r in (1, 7, 2, 6):
                stat_send(r).wait_recv()
            own = [run[0, n : n + 1, :] for n in range(3)]
            pack(0, own)
            merged = merge([sto[0]] + [sti[32 + r] for r in (1, 7, 2, 6)])
            for n in range(3):
                sto[0, 2 * n : 2 * n + 2, :] = merged[n]
            for d in (4, 3, 5, 2, 6, 1, 7):
                total_send(0, d).start()
            prepare_queries(4)

        r = jnp.where(i % 2 == 1, (i + 1) // 2, (8 - i // 2) % 8)

        @pl.when(i >= 3)
        def _():
            near_piece(r)

        @pl.when(x >= 1)
        def _():
            piece(r, 1, [(1, 1), (2, 2)])

        @pl.when(i > 0)
        def _():
            pack(r, [run[r, n : n + 1, :] for n in range(3)])

        @pl.when((i > 0) & (i < 5))
        def _():
            stat_send(r).start()

        return 0

    lax.fori_loop(0, Z, block, 0)
    for kind in (3, 1, 2):
        for d in (4, 3, 5, 2, 6, 1, 7):
            total_send(kind, d).start()

    def all_products(i, _):
        products((i + 4) % Z)
        return 0

    lax.fori_loop(0, Z, all_products, 0)

    pltpu.make_async_copy(
        sti.at[pl.ds(0, 4 * (Z - 1))], sti.at[pl.ds(0, 4 * (Z - 1))], fn_r.at[0]
    ).wait()
    for r in range(Z):
        parts = [sto[0] if r == 0 else sti[r]]
        for kind in (1, 2, 3):
            parts.append(sto[r] if far_blocks[kind - 1] == r else sti[kind * Z + r])
        top, total, moment = merge(parts)
        inverse = 1.0 / total
        for n, value in enumerate((top, inverse, moment * inverse)):
            fin[r, n : n + 1, :] = jnp.concatenate([value[0:1, :], value[1:2, :]], axis=1)

    def z_sum(d, i, what, h):
        return copy(
            zs.at[d, i, what, h], zr.at[d, i, what, h], za_s.at[d, i, what, h], za_r.at[d, i, what, h],
            z_right if d == 0 else z_left,
        )

    def z_part(r, what, h):
        rows = slice(h * 64, (h + 1) * 64)
        later = slice(HD + h * 64, HD + (h + 1) * 64)
        scale = jnp.exp2((run[r, 0:1, :] - fin[r, 0:1, :]) * ALPHA) * fin[r, 1:2, :]
        if what == 0:
            return accv[r, rows, :] * scale
        return (accw[r, rows, :] - fin[r, 2:3, :] * accv[r, later, :]) * (scale * INV_ROOT)

    def z_add(i):
        for what in range(2):
            for h in range(2):
                for d in range(2):
                    r = 4 + i if d == 0 else 4 - i
                    if i == 0 and what != d:
                        continue
                    part = z_part(r, what, h)
                    if i > 1 or (i == 1 and what == d):
                        z_sum(d, i - 1, what, h).wait_recv()
                        part = part + zr[d, i - 1, what, h].astype(F32)
                    zs[d, i, what, h] = part.astype(BF16)
                    send(z_sum(d, i, what, h))

    def sib_send(s):
        return copy(sbs.at[s], sbr.at[s], sb_s.at[s], sb_r.at[s], sib)

    mine = pl.ds(pl.multiple_of(core * T, T), T)
    other = pl.ds(pl.multiple_of((1 - core) * T, T), T)

    def factors(r, which):
        scale = jnp.exp2((pst[r, which, 0:1, :] - fin[r, 0:1, :]) * ALPHA) * fin[r, 1:2, :]
        root = scale * INV_ROOT
        shift = root * (pst[r, which, 1:2, :] - fin[r, 2:3, :])
        q = qt[r].astype(F32)
        return (
            (gt[r].astype(F32) * scale).astype(BF16),
            (q * shift).astype(BF16),
            (q * root).astype(BF16),
        )

    def sib_half(s):
        sbs[s] = kacc[s, :, other].astype(BF16)
        send(sib_send(s))

    def far_key(s):
        kacc[s] = jnp.zeros((2 * HD, C), F32)

        @pl.when(x >= s)
        def _():
            rows = slice(s * C, (s + 1) * C)
            kacc[s] = dot_nt(left_e[...], eb[rows, :])
            kacc[s, HD:, :] += dot_nt(left_t[...], tb[rows, :])

        sib_half(s)

    def near_key(s, r_low, r_high):
        kacc[s] = jnp.zeros((2 * HD, C), F32)

        def body(i, _):
            r = i % Z
            lanes = block_lanes(r)
            g_scaled, q_shift, q_root = factors(r, 0)
            sum_e = dot_nt(jnp.concatenate([g_scaled, q_shift], axis=0), eb[0:C, lanes])
            sum_t = dot_nt(q_root, tb[0:C, lanes])
            kacc[s, 0:HD, :] += sum_e[0:HD, :]
            kacc[s, HD:, :] += sum_e[HD:, :] + sum_t
            return 0

        lax.fori_loop(r_low, r_high, body, 0)
        sib_half(s)

    def own_part(s, what):
        rows = slice(what * HD, (what + 1) * HD)
        return kacc[s, rows, mine] + sbr[s, rows, :].astype(F32)

    x_target = [x_right, x_left, x_left, x_left, x_right, x_right]

    def x_sum(i):
        return copy(xs.at[i], xr.at[i], xr_s.at[i], xr_r.at[i], x_target[i])

    def x_send(i, part):
        xs[i] = part.astype(BF16)
        send(x_sum(i))

    z_add(0)

    @pl.when(x >= 1)
    def _():
        def scale_left(r, _):
            lanes = block_lanes(r)
            left_e[0:HD, lanes], left_e[HD:, lanes], left_t[:, lanes] = factors(r, 1)
            return 0

        lax.fori_loop(0, Z, scale_left, 0)

    far_key(2)
    far_key(1)
    sib_send(2).wait_recv()
    x_send(0, own_part(2, 0))
    x_send(1, own_part(2, 1))
    z_add(1)
    near_key(3, 4, jnp.where(x == X - 1, z + 1, 4))
    sib_send(1).wait_recv()
    x_send(2, own_part(1, 0))
    sib_send(3).wait_recv()
    x_send(5, own_part(3, 1))
    z_add(2)
    near_key(0, z + 1, Z + 1)
    x_sum(1).wait_recv()
    x_send(3, own_part(1, 1) + xr[1].astype(F32))
    x_sum(0).wait_recv()
    x_send(4, own_part(3, 0) + xr[0].astype(F32))
    z_add(3)
    sib_send(0).wait_recv()
    for what, near in ((0, (2, 4)), (1, (3, 5))):
        part = own_part(0, what)
        for i in near:
            x_sum(i).wait_recv()
            part = part + xr[i].astype(F32)
        out_ref[3 - what] = part.T.astype(BF16)

    for what in range(2):
        halves = []
        for h in range(2):
            part = z_part(0, what, h)
            for d in range(2):
                z_sum(d, 3, what, h).wait_recv()
                part = part + zr[d, 3, what, h].astype(F32)
            halves.append(part)
        out_ref[what] = jnp.concatenate(halves, axis=0).T.astype(BF16)

    for hops in (*q_right, *q_left, *g_right, *g_left):
        for op in hops:
            op.wait_send()
    for op in (*k_sib, *v_sib, k_right, v_right, k_left, v_left, k_far, v_far, *started):
        op.wait_send()
    for r in (1, 7, 2, 6):
        stat_send(r).wait_send()
    pltpu.make_async_copy(
        sti.at[pl.ds(0, 4 * (Z - 1))], sti.at[pl.ds(0, 4 * (Z - 1))], fn_s.at[0]
    ).wait()


def hand_on(all_ref, *outs):
    for i, out in enumerate(outs):
        out[...] = all_ref[i]


def per_device(queries, keys, values, out_grad, segments):
    vmem = pl.BlockSpec(memory_space=pltpu.VMEM)
    dma = pltpu.SemaphoreType.DMA
    sums = pl.pallas_call(
        kernel,
        out_shape=jax.ShapeDtypeStruct((4, T, HD), BF16),
        in_specs=[vmem] * 5,
        out_specs=vmem,
        scratch_shapes=[
            pltpu.VMEM((SEG_ROWS, HD), F32),
            pltpu.VMEM((Z, T + SEG_ROWS, HD), BF16),
            pltpu.VMEM((Z, T, HD), BF16),
            pltpu.VMEM((Z, HD, T), BF16),
            pltpu.VMEM((Z, HD, T), BF16),
            pltpu.VMEM((X, 2, T + SEG_ROWS, HD), BF16),
            pltpu.VMEM((X, 2, T, HD), BF16),
            pltpu.VMEM((2 * HD, X * C), BF16),
            pltpu.VMEM((3 * C, Z * T), BF16),
            pltpu.VMEM((3 * C, Z * T), BF16),
            pltpu.VMEM((4, T, T), F32),
            pltpu.VMEM((4, T, T), F32),
            pltpu.VMEM((Z, 2, 8, T), F32),
            pltpu.VMEM((Z, 8, T), F32),
            pltpu.VMEM((Z, 2 * HD, T), F32),
            pltpu.VMEM((Z, HD, T), F32),
            pltpu.VMEM((2 * HD, Z * T), BF16),
            pltpu.VMEM((HD, Z * T), BF16),
            pltpu.VMEM((X, 2 * HD, C), F32),
            pltpu.VMEM((X, 16, T), F32),
            pltpu.VMEM((Z, 8, HD), F32),
            pltpu.VMEM((5 * Z, 8, HD), F32),
            pltpu.VMEM((Z, 8, T), F32),
            pltpu.VMEM((2, 4, 2, 2, HD // 2, T), BF16),
            pltpu.VMEM((2, 4, 2, 2, HD // 2, T), BF16),
            pltpu.VMEM((X, 2 * HD, T), BF16),
            pltpu.VMEM((X, 2 * HD, T), BF16),
            pltpu.VMEM((6, HD, T), BF16),
            pltpu.VMEM((6, HD, T), BF16),
            dma((Z, 2)), dma((Z, 2)), dma((Z, 2)), dma((Z, 2)),
            dma((14,)), dma((14,)),
            dma((Z,)), dma((Z,)), dma((1,)), dma((1,)),
            dma((2, 4, 2, 2)), dma((2, 4, 2, 2)),
            dma((X,)), dma((X,)), dma((6,)), dma((6,)),
        ],
        compiler_params=pltpu.CompilerParams(
            collective_id=0, has_side_effects=True, vmem_limit_bytes=44 * 1024 * 1024
        ),
        cost_estimate=pl.CostEstimate(
            flops=4 * 10**9, bytes_accessed=600_000, transcendentals=2 * 10**6
        ),
    )(queries, keys, values, out_grad, segments.reshape(T // HD, HD))
    return pl.pallas_call(
        hand_on,
        out_shape=(jax.ShapeDtypeStruct((T, HD), BF16),) * 4,
        in_specs=[vmem],
        out_specs=(vmem,) * 4,
    )(sums)


def solution(mesh):
    rows = P(("dp", "ctx"), None)
    return jax.shard_map(
        per_device,
        mesh=mesh,
        in_specs=(rows, rows, rows, rows, P(("dp", "ctx"))),
        out_specs=(rows, rows, rows, rows),
        check_vma=False,
    )
```

time: 61 us -> 56.3 us (0.923)
  the two profiles are of different devices: /device:TPU:1 before, /device:TPU:8 now
where the time goes in v3:
time: 56.3 us; the launch traced here: 56 us
  Pallas kernels  50.6 us (90%)
  local copies, waits for them, and re-layouts  4.72 us (8%)
  between operations  0.66 us (1%)
    pallas_call x1, Pallas kernels, per_device(): pl.pallas_call(kernel, out_shape=jax.ShapeDtypeStruct((4, T, HD), BF16),...  48.9 us
    unnamed x12, local copies, waits for them, and re-layouts  4.72 us
    pallas_call x1, Pallas kernels, per_device(): pl.pallas_call(hand_on, out_shape=(jax.ShapeDtypeStruct((T, HD), BF16),)...  1.65 us

profile of v3, /device:TPU:8, one launch (start us, length us, event | category | flops | bytes accessed | tf_op | source)
XLA Modules:
  0.0 56.0 jit_solution(14979598978965377191)
XLA Ops:
  0.6 0.0 copy-start.5
  0.6 0.7 %copy-done.5 = s32[256]{0:T(256)S(1)} copy-done((s32[256]{0:T(256)S(1)}, s32[256]{0:T(256)}, u32[]{:S(2)}) %copy-start.5) | copy-done | bytes 1048
  1.3 0.0 copy-start.1
  1.3 0.8 %copy-done.1 = bf16[256,128]{1,0:T(8,128)(2,1)S(1)} copy-done((bf16[256,128]{1,0:T(8,128)(2,1)S(1)}, bf16[256,128]{1,0:T(8,128)(2,1)}, u32[]{:S(2)}) %copy-start.1) | copy-done | bytes 65560
  2.2 0.0 copy-start.2
  2.2 0.8 %copy-done.2 = bf16[256,128]{1,0:T(8,128)(2,1)S(1)} copy-done((bf16[256,128]{1,0:T(8,128)(2,1)S(1)}, bf16[256,128]{1,0:T(8,128)(2,1)}, u32[]{:S(2)}) %copy-start.2) | copy-done | bytes 65560
  3.0 0.0 copy-start.3
  3.0 0.8 %copy-done.3 = bf16[256,128]{1,0:T(8,128)(2,1)S(1)} copy-done((bf16[256,128]{1,0:T(8,128)(2,1)S(1)}, bf16[256,128]{1,0:T(8,128)(2,1)}, u32[]{:S(2)}) %copy-start.3) | copy-done | bytes 65560
  3.8 0.0 copy-start.4
  3.8 0.8 %copy-done.4 = bf16[256,128]{1,0:T(8,128)(2,1)S(1)} copy-done((bf16[256,128]{1,0:T(8,128)(2,1)S(1)}, bf16[256,128]{1,0:T(8,128)(2,1)}, u32[]{:S(2)}) %copy-start.4) | copy-done | bytes 65560
  4.7 48.9 %shard_map.84.all_ref = bf16[4,256,128]{2,1,0:T(8,128)(2,1)S(1)} custom-call(bf16[256,128]{1,0:T(8,128)(2,1)S(1)} %copy-done.1, bf16[256,128]{1,0:T(8,128)(2,1)S(1)} %copy-done.2, bf16[256,128]{1,0:T(8,128)(2,1)S(1)} %copy-done.3, bf16[256,128]{1,0:T(8,128)(2,1)S(1)} %copy-done.4, s32[2,128]{1,0:T(2,128)S(1)} %bitcast.1), custom_call_target="tpu_custom_call" | custom-call | flops 4000000000 | bytes 600000 | tf_op jit(solution)/shard_map/pallas_call | solution.py:525
  53.6 0.0 copy-start
  53.6 0.7 %copy-done = bf16[4,256,128]{2,1,0:T(8,128)(2,1)} copy-done((bf16[4,256,128]{2,1,0:T(8,128)(2,1)}, bf16[4,256,128]{2,1,0:T(8,128)(2,1)S(1)}, u32[]{:S(2)}) %copy-start) | copy-done | bytes 262168
  54.3 1.6 %shard_map.85 = (bf16[256,128]{1,0:T(8,128)(2,1)}, bf16[256,128]{1,0:T(8,128)(2,1)}, bf16[256,128]{1,0:T(8,128)(2,1)}, bf16[256,128]{1,0:T(8,128)(2,1)}) custom-call(bf16[4,256,128]{2,1,0:T(8,128)(2,1)} %copy-done), custom_call_target="tpu_custom_call" | custom-call | tf_op jit(solution)/shard_map/pallas_call | solution.py:573
Async XLA Ops:
  0.6 0.7 %copy-start.5 = (s32[256]{0:T(256)S(1)}, s32[256]{0:T(256)}, u32[]{:S(2)}) copy-start(s32[256]{0:T(256)} %param.9) | copy-start | bytes 3076
  1.3 0.8 %copy-start.1 = (bf16[256,128]{1,0:T(8,128)(2,1)S(1)}, bf16[256,128]{1,0:T(8,128)(2,1)}, u32[]{:S(2)}) copy-start(bf16[256,128]{1,0:T(8,128)(2,1)} %q_ref.1) | copy-start | bytes 196612
  2.2 0.8 %copy-start.2 = (bf16[256,128]{1,0:T(8,128)(2,1)S(1)}, bf16[256,128]{1,0:T(8,128)(2,1)}, u32[]{:S(2)}) copy-start(bf16[256,128]{1,0:T(8,128)(2,1)} %k_ref.1) | copy-start | bytes 196612
  3.0 0.8 %copy-start.3 = (bf16[256,128]{1,0:T(8,128)(2,1)S(1)}, bf16[256,128]{1,0:T(8,128)(2,1)}, u32[]{:S(2)}) copy-start(bf16[256,128]{1,0:T(8,128)(2,1)} %v_ref.1) | copy-start | bytes 196612
  3.8 0.8 %copy-start.4 = (bf16[256,128]{1,0:T(8,128)(2,1)S(1)}, bf16[256,128]{1,0:T(8,128)(2,1)}, u32[]{:S(2)}) copy-start(bf16[256,128]{1,0:T(8,128)(2,1)} %g_ref.1) | copy-start | bytes 196612
  53.6 0.7 %copy-start = (bf16[4,256,128]{2,1,0:T(8,128)(2,1)}, bf16[4,256,128]{2,1,0:T(8,128)(2,1)S(1)}, u32[]{:S(2)}) copy-start(bf16[4,256,128]{2,1,0:T(8,128)(2,1)S(1)} %shard_map.84.all_ref) | copy-start | bytes 786436

commit v4 on v3

--- a/solution.py
+++ b/solution.py
@@ -30,12 +30,19 @@
     return jnp.dot(a, b, preferred_element_type=F32)
 
 
+def pick(index, values):
+    result = values[-1]
+    for i in range(len(values) - 2, -1, -1):
+        result = jnp.where(index == i, values[i], result)
+    return result
+
+
 def kernel(
     q_ref, k_ref, v_ref, g_ref, seg_ref, out_ref,
-    segf, qs, gs, qt, gt, ks, vs, vkt, eb, tb, sbuf, dbuf, pst, run, accv, accw,
+    segi, segf, out_v, qs, gs, qt, gt, ks, vs, vkt, eb, tb, sbuf, dbuf, pst, run, accv, accw,
     left_e, left_t, kacc, cnt, sto, sti, fin, zs, zr, sbs, sbr, xs, xr,
     zq_s, zq_r, zg_s, zg_r, kv_s, kv_r, st_s, st_r, fn_s, fn_r,
-    za_s, za_r, sb_s, sb_r, xr_s, xr_r,
+    za_s, za_r, sb_s, sb_r, xr_s, xr_r, in_s, out_s,
 ):
     ctx = lax.axis_index("ctx")
     x = ctx // (2 * Z)
@@ -53,15 +60,29 @@
     for peer in (z_right, z_left, x_right, x_left, sib):
         pl.semaphore_signal(barrier, inc=1, device_id=peer, device_id_type=MESH)
 
+    loads = [
+        pltpu.make_async_copy(src, dst, in_s.at[i])
+        for i, (src, dst) in enumerate((
+            (seg_ref, segi),
+            (q_ref, qs.at[0, 0:T, :]),
+            (k_ref, ks.at[0, core, 0:T, :]),
+            (v_ref, vs.at[0, core]),
+            (g_ref, gs.at[0]),
+        ))
+    ]
+    for op in loads:
+        op.start()
     segf[...] = jnp.zeros_like(segf)
-    segf[0 : T // HD, :] = seg_ref[...].astype(F32)
+    for r in range(Z):
+        run[r, 0:1, :] = jnp.full((1, T), NEG, F32)
+        run[r, 1:8, :] = jnp.zeros((7, T), F32)
+    loads[0].wait()
+    segf[0 : T // HD, :] = segi[...].astype(F32)
     seg_rows = segf[...].astype(BF16)
-    qs[0, 0:T, :] = q_ref[...]
     qs[0, T : T + SEG_ROWS, :] = seg_rows
-    gs[0] = g_ref[...]
-    ks[0, core, 0:T, :] = k_ref[...]
     ks[0, core, T : T + SEG_ROWS, :] = seg_rows
-    vs[0, core] = v_ref[...]
+    for op in loads[1:]:
+        op.wait()
 
     pl.semaphore_wait(barrier, 5)
 
@@ -105,20 +126,19 @@
     k_far, v_far = k_hop(12, 1, 2, x_right), v_hop(13, 3, 2, x_left)
 
     for op in (
-        q_right[0][0], q_left[0][0], k_right, k_left, k_sib[0], v_sib[0],
-        q_right[0][1], q_left[0][1], v_left, v_right,
+        q_right[0][0], q_left[0][0], k_right, v_left, k_sib[0], v_sib[0],
+        q_right[0][1], q_left[0][1], v_right, k_left,
         g_right[0][0], g_left[0][0], g_right[0][1], g_left[0][1],
     ):
         op.start()
 
-    def z_step(j):
-        for right, left in ((q_right, q_left), (g_right, g_left)):
-            for h in range(2):
-                for hops in (right, left):
-                    if j <= len(hops):
-                        hops[j - 1][h].wait_recv()
-                    if j < len(hops):
-                        hops[j][h].start()
+    def z_step(j, what):
+        for h in range(2):
+            for hops in ((q_right, q_left), (g_right, g_left))[what]:
+                if j <= len(hops):
+                    hops[j - 1][h].wait_recv()
+                if j < len(hops):
+                    hops[j][h].start()
 
     doc16 = lax.broadcasted_iota(jnp.int32, (16, HD), 0).astype(F32)
 
@@ -224,10 +244,6 @@
         def _():
             add_part(1, slice(C, 3 * C), slice(C, 3 * C))
 
-    for r in range(Z):
-        run[r, 0:1, :] = jnp.full((1, T), NEG, F32)
-        run[r, 1:8, :] = jnp.zeros((7, T), F32)
-
     def pack(i, values):
         for n in range(3):
             for h in range(2):
@@ -256,62 +272,60 @@
     prepare_keys(0)
     piece(0, 0, [(0, 0)], diagonal=True)
 
+    z_step(1, 0)
     k_right.wait_recv()
     k_far.start()
     k_sib[1].start()
-    for h in range(2):
-        q_right[0][h].wait_recv()
-        q_right[1][h].start()
-        q_left[0][h].wait_recv()
-        q_left[1][h].start()
-    k_left.wait_recv()
-    k_sib[3].start()
     v_left.wait_recv()
     v_far.start()
     v_sib[3].start()
+    z_step(1, 1)
     v_right.wait_recv()
     v_sib[1].start()
-    for h in range(2):
-        g_right[0][h].wait_recv()
-        g_right[1][h].start()
-        g_left[0][h].wait_recv()
-        g_left[1][h].start()
+    k_left.wait_recv()
+    k_sib[3].start()
     prepare_queries(1)
     prepare_queries(7)
+    z_step(2, 0)
     for s in (1, 3):
         k_sib[s].wait_recv()
         v_sib[s].wait_recv()
         prepare_keys(s)
     k_far.wait_recv()
     k_sib[2].start()
-
-    def early(i, _):
-        near_piece(jnp.where(i == 0, 1, 7))
-        return 0
-
-    lax.fori_loop(0, 2, early, 0)
-    z_step(2)
     v_far.wait_recv()
     v_sib[2].start()
-    prepare_queries(2)
-    prepare_queries(6)
+
+    def early(i, _):
+        @pl.when(i == 1)
+        def _():
+            z_step(2, 1)
+            prepare_queries(2)
+            prepare_queries(6)
+
+        near_piece(pick(i, [1, 7, 2, 6]))
+        return 0
+
+    lax.fori_loop(0, 4, early, 0)
     k_sib[2].wait_recv()
     v_sib[2].wait_recv()
     prepare_keys(2)
 
     def block(i, _):
+        @pl.when(i == 1)
+        def _():
+            z_step(3, 0)
+
         @pl.when(i == 3)
         def _():
-            z_step(3)
-
-        @pl.when(i == 5)
-        def _():
+            z_step(3, 1)
             prepare_queries(3)
             prepare_queries(5)
 
         @pl.when(i == 7)
         def _():
-            z_step(4)
+            z_step(4, 0)
+            z_step(4, 1)
             for r in (1, 7, 2, 6):
                 stat_send(r).wait_recv()
             own = [run[0, n : n + 1, :] for n in range(3)]
@@ -319,13 +333,14 @@
             merged = merge([sto[0]] + [sti[32 + r] for r in (1, 7, 2, 6)])
             for n in range(3):
                 sto[0, 2 * n : 2 * n + 2, :] = merged[n]
-            for d in (4, 3, 5, 2, 6, 1, 7):
-                total_send(0, d).start()
+            for kind in (1, 2, 0):
+                for d in (4, 3, 5, 2, 6, 1, 7):
+                    total_send(kind, d).start()
             prepare_queries(4)
 
         r = jnp.where(i % 2 == 1, (i + 1) // 2, (8 - i // 2) % 8)
 
-        @pl.when(i >= 3)
+        @pl.when(i >= 5)
         def _():
             near_piece(r)
 
@@ -344,9 +359,8 @@
         return 0
 
     lax.fori_loop(0, Z, block, 0)
-    for kind in (3, 1, 2):
-        for d in (4, 3, 5, 2, 6, 1, 7):
-            total_send(kind, d).start()
+    for d in (4, 3, 5, 2, 6, 1, 7):
+        total_send(3, d).start()
 
     def all_products(i, _):
         products((i + 4) % Z)
@@ -380,15 +394,14 @@
             return accv[r, rows, :] * scale
         return (accw[r, rows, :] - fin[r, 2:3, :] * accv[r, later, :]) * (scale * INV_ROOT)
 
-    def z_add(i):
-        for what in range(2):
+    def z_add(i, order=(1, 0)):
+        for short in order:
             for h in range(2):
                 for d in range(2):
+                    what = 1 - d if short else d
                     r = 4 + i if d == 0 else 4 - i
-                    if i == 0 and what != d:
-                        continue
                     part = z_part(r, what, h)
-                    if i > 1 or (i == 1 and what == d):
+                    if i > short:
                         z_sum(d, i - 1, what, h).wait_recv()
                         part = part + zr[d, i - 1, what, h].astype(F32)
                     zs[d, i, what, h] = part.astype(BF16)
@@ -455,7 +468,8 @@
         xs[i] = part.astype(BF16)
         send(x_sum(i))
 
-    z_add(0)
+    z_add(0, (0,))
+    z_add(1, (1,))
 
     @pl.when(x >= 1)
     def _():
@@ -471,7 +485,7 @@
     sib_send(2).wait_recv()
     x_send(0, own_part(2, 0))
     x_send(1, own_part(2, 1))
-    z_add(1)
+    z_add(1, (0,))
     near_key(3, 4, jnp.where(x == X - 1, z + 1, 4))
     sib_send(1).wait_recv()
     x_send(2, own_part(1, 0))
@@ -484,13 +498,31 @@
     x_sum(0).wait_recv()
     x_send(4, own_part(3, 0) + xr[0].astype(F32))
     z_add(3)
+
+    def leave(i):
+        return pltpu.make_async_copy(out_v.at[i], out_ref.at[i], out_s.at[i])
+
     sib_send(0).wait_recv()
     for what, near in ((0, (2, 4)), (1, (3, 5))):
         part = own_part(0, what)
         for i in near:
             x_sum(i).wait_recv()
             part = part + xr[i].astype(F32)
-        out_ref[3 - what] = part.T.astype(BF16)
+        out_v[3 - what] = part.T.astype(BF16)
+        leave(3 - what).start()
+
+    for hops in (*q_right, *q_left, *g_right, *g_left):
+        for op in hops:
+            op.wait_send()
+    for op in (*k_sib, *v_sib, k_right, v_right, k_left, v_left, k_far, v_far):
+        op.wait_send()
+    for r in (1, 7, 2, 6):
+        stat_send(r).wait_send()
+    pltpu.make_async_copy(
+        sti.at[pl.ds(0, 4 * (Z - 1))], sti.at[pl.ds(0, 4 * (Z - 1))], fn_s.at[0]
+    ).wait()
+    for op in started:
+        op.wait_send()
 
     for what in range(2):
         halves = []
@@ -500,18 +532,10 @@
                 z_sum(d, 3, what, h).wait_recv()
                 part = part + zr[d, 3, what, h].astype(F32)
             halves.append(part)
-        out_ref[what] = jnp.concatenate(halves, axis=0).T.astype(BF16)
-
-    for hops in (*q_right, *q_left, *g_right, *g_left):
-        for op in hops:
-            op.wait_send()
-    for op in (*k_sib, *v_sib, k_right, v_right, k_left, v_left, k_far, v_far, *started):
-        op.wait_send()
-    for r in (1, 7, 2, 6):
-        stat_send(r).wait_send()
-    pltpu.make_async_copy(
-        sti.at[pl.ds(0, 4 * (Z - 1))], sti.at[pl.ds(0, 4 * (Z - 1))], fn_s.at[0]
-    ).wait()
+        out_v[what] = jnp.concatenate(halves, axis=0).T.astype(BF16)
+        leave(what).start()
+    for i in range(4):
+        leave(i).wait()
 
 
 def hand_on(all_ref, *outs):
@@ -520,15 +544,18 @@
 
 
 def per_device(queries, keys, values, out_grad, segments):
+    place = pl.BlockSpec(memory_space=pl.ANY)
     vmem = pl.BlockSpec(memory_space=pltpu.VMEM)
     dma = pltpu.SemaphoreType.DMA
     sums = pl.pallas_call(
         kernel,
         out_shape=jax.ShapeDtypeStruct((4, T, HD), BF16),
-        in_specs=[vmem] * 5,
-        out_specs=vmem,
+        in_specs=[place] * 5,
+        out_specs=place,
         scratch_shapes=[
+            pltpu.VMEM((T // HD, HD), jnp.int32),
             pltpu.VMEM((SEG_ROWS, HD), F32),
+            pltpu.VMEM((4, T, HD), BF16),
             pltpu.VMEM((Z, T + SEG_ROWS, HD), BF16),
             pltpu.VMEM((Z, T, HD), BF16),
             pltpu.VMEM((Z, HD, T), BF16),
@@ -561,10 +588,10 @@
             dma((14,)), dma((14,)),
             dma((Z,)), dma((Z,)), dma((1,)), dma((1,)),
             dma((2, 4, 2, 2)), dma((2, 4, 2, 2)),
-            dma((X,)), dma((X,)), dma((6,)), dma((6,)),
+            dma((X,)), dma((X,)), dma((6,)), dma((6,)), dma((5,)), dma((4,)),
         ],
         compiler_params=pltpu.CompilerParams(
-            collective_id=0, has_side_effects=True, vmem_limit_bytes=44 * 1024 * 1024
+            collective_id=0, has_side_effects=True, vmem_limit_bytes=58 * 1024 * 1024
         ),
         cost_estimate=pl.CostEstimate(
             flops=4 * 10**9, bytes_accessed=600_000, transcendentals=2 * 10**6

time: 56.3 us -> 51.4 us (0.913)
  local copies, waits for them, and re-layouts: 4.72 us -> 0 us
    unnamed x12 -> x0, local copies, waits for them, and re-layouts: 4.72 us -> none
where the time goes in v4:
time: 51.4 us; the launch traced here: 51.2 us
  Pallas kernels  50.6 us (98%)
  between operations  0.64 us (1%)
    pallas_call x1, Pallas kernels, per_device(): pl.pallas_call(kernel, out_shape=jax.ShapeDtypeStruct((4, T, HD), BF16),...  49 us
    pallas_call x1, Pallas kernels, per_device(): pl.pallas_call(hand_on, out_shape=(jax.ShapeDtypeStruct((T, HD), BF16),)...  1.65 us

profile of v4, /device:TPU:8, one launch (start us, length us, event | category | flops | bytes accessed | tf_op | source)
XLA Modules:
  0.0 51.2 jit_solution(8898444056691840772)
XLA Ops:
  0.6 49.0 %shard_map.84.all_ref = bf16[4,256,128]{2,1,0:T(8,128)(2,1)} custom-call(bf16[256,128]{1,0:T(8,128)(2,1)} %q_ref.1, bf16[256,128]{1,0:T(8,128)(2,1)} %k_ref.1, bf16[256,128]{1,0:T(8,128)(2,1)} %v_ref.1, bf16[256,128]{1,0:T(8,128)(2,1)} %g_ref.1, s32[2,128]{1,0:T(2,128)} %bitcast.1), custom_call_target="tpu_custom_call" | custom-call | flops 4000000000 | bytes 600000 | tf_op jit(solution)/shard_map/pallas_call | solution.py:550
  49.6 1.7 %shard_map.85 = (bf16[256,128]{1,0:T(8,128)(2,1)}, bf16[256,128]{1,0:T(8,128)(2,1)}, bf16[256,128]{1,0:T(8,128)(2,1)}, bf16[256,128]{1,0:T(8,128)(2,1)}) custom-call(bf16[4,256,128]{2,1,0:T(8,128)(2,1)} %shard_map.84.all_ref), custom_call_target="tpu_custom_call" | custom-call | tf_op jit(solution)/shard_map/pallas_call | solution.py:600

commit v5 on v4

v5 whole, which is shorter than its diff:
```python
import functools
import math

import jax
import jax.numpy as jnp
from jax import lax
from jax.experimental import pallas as pl
from jax.experimental.pallas import tpu as pltpu
from jax.sharding import PartitionSpec as P

MESH = pl.DeviceIdType.MESH
HD = 128
X, Z = 4, 8
T = 256
C = 2 * T
SEG_ROWS = 16
NEG = -1e30
INV_ROOT = 1.0 / math.sqrt(HD)
ALPHA = INV_ROOT * math.log2(math.e)
F32 = jnp.float32
BF16 = jnp.bfloat16
NT = (((1,), (1,)), ((), ()))


def dot_nt(a, b):
    return lax.dot_general(a, b, NT, preferred_element_type=F32)


def dot(a, b):
    return jnp.dot(a, b, preferred_element_type=F32)


def pick(index, values):
    result = values[-1]
    for i in range(len(values) - 2, -1, -1):
        result = jnp.where(index == i, values[i], result)
    return result


def kernel(
    q_ref, k_ref, v_ref, g_ref, seg_ref, out_ref,
    segi, segf, out_v, qs, gs, qt, gt, ks, vs, vkt, eb, tb, sbuf, dbuf, pst, run, accv, accw,
    left_e, left_t, kacc, cnt, sto, sti, fin, zs, zr, sbs, sbr, xs, xr,
    zq_s, zq_r, zg_s, zg_r, kv_s, kv_r, st_s, st_r, fn_s, fn_r,
    za_s, za_r, sb_s, sb_r, xr_s, xr_r, in_s, out_s,
):
    ctx = lax.axis_index("ctx")
    x = ctx // (2 * Z)
    z = (ctx // 2) % Z
    core = ctx % 2

    def dev(xx, zz, cc):
        return {"ctx": ((xx + X) % X) * (2 * Z) + ((zz + Z) % Z) * 2 + cc}

    sib = dev(x, z, 1 - core)
    z_right, z_left = dev(x, z + 1, core), dev(x, z - 1, core)
    x_right, x_left = dev(x + 1, z, core), dev(x - 1, z, core)

    barrier = pltpu.get_barrier_semaphore()
    for peer in (z_right, z_left, x_right, x_left, sib):
        pl.semaphore_signal(barrier, inc=1, device_id=peer, device_id_type=MESH)

    loads = [
        pltpu.make_async_copy(src, dst, in_s.at[i])
        for i, (src, dst) in enumerate((
            (seg_ref, segi),
            (q_ref, qs.at[0, 0:T, :]),
            (k_ref, ks.at[0, core, 0:T, :]),
            (v_ref, vs.at[0, core]),
            (g_ref, gs.at[0]),
        ))
    ]
    for op in loads:
        op.start()
    segf[...] = jnp.zeros_like(segf)
    run[0:1, :] = jnp.full((1, Z * T), NEG, F32)
    run[1:8, :] = jnp.zeros((7, Z * T), F32)
    loads[0].wait()
    segf[0 : T // HD, :] = segi[...].astype(F32)
    seg_rows = segf[...].astype(BF16)
    qs[0, T : T + SEG_ROWS, :] = seg_rows
    ks[0, core, T : T + SEG_ROWS, :] = seg_rows
    for op in loads[1:]:
        op.wait()

    pl.semaphore_wait(barrier, 5)

    def copy(src, dst, send, recv, target):
        return pltpu.make_async_remote_copy(
            src_ref=src, dst_ref=dst, send_sem=send, recv_sem=recv,
            device_id=target, device_id_type=MESH,
        )

    started = []

    def send(op):
        op.start()
        started.append(op)

    half = (slice(0, T + SEG_ROWS),)

    def q_hop(src, dst, target, h):
        return copy(
            qs.at[src, half[h], :], qs.at[dst, half[h], :], zq_s.at[dst, h], zq_r.at[dst, h], target
        )

    def g_hop(src, dst, target, h):
        rows = slice(h * 256, (h + 1) * 256)
        return copy(gs.at[src, rows, :], gs.at[dst, rows, :], zg_s.at[dst, h], zg_r.at[dst, h], target)

    def k_hop(i, src, dst, target):
        return copy(ks.at[src, core], ks.at[dst, core], kv_s.at[i], kv_r.at[i], target)

    def v_hop(i, src, dst, target):
        return copy(vs.at[src, core], vs.at[dst, core], kv_s.at[i], kv_r.at[i], target)

    q_right = [[q_hop(j, j + 1, z_right, h) for h in range(1)] for j in range(4)]
    q_left = [[q_hop((8 - j) % 8, 7 - j, z_left, h) for h in range(1)] for j in range(3)]
    g_right = [[g_hop(j, j + 1, z_right, h) for h in range(1)] for j in range(3)]
    g_left = [[g_hop((8 - j) % 8, 7 - j, z_left, h) for h in range(1)] for j in range(4)]
    k_sib = [k_hop(s, s, s, sib) for s in range(4)]
    v_sib = [v_hop(4 + s, s, s, sib) for s in range(4)]
    k_right, v_right = k_hop(8, 0, 1, x_right), v_hop(9, 0, 1, x_right)
    k_left, v_left = k_hop(10, 0, 3, x_left), v_hop(11, 0, 3, x_left)
    k_far, v_far = k_hop(12, 1, 2, x_right), v_hop(13, 3, 2, x_left)

    for op in (q_right[0][0], g_left[0][0], k_right, v_left, k_sib[0], v_sib[0]):
        op.start()
    for h in range(1, 1):
        q_right[0][h].start()
        g_left[0][h].start()
    v_right.start()
    k_left.start()
    for h in range(1):
        g_right[0][h].start()
        q_left[0][h].start()

    def z_step(j, which):
        for h in range(1):
            for hops in ((q_right, g_left), (g_right, q_left))[which]:
                if j <= len(hops):
                    hops[j - 1][h].wait_recv()
                if j < len(hops):
                    hops[j][h].start()

    doc16 = lax.broadcasted_iota(jnp.int32, (16, HD), 0).astype(F32)

    def prepare_keys(s):
        below = jnp.zeros((16, HD), F32)
        for c in range(2):
            lanes = slice(s * C + c * T, s * C + (c + 1) * T)
            vkt[0:HD, lanes] = vs[s, c].T
            vkt[HD:, lanes] = ks[s, c, 0:T, :].T
            seg = ks[s, c, T : T + SEG_ROWS, :].astype(F32)
            for h in range(T // HD):
                below += jnp.where(seg[h : h + 1, :] < doc16, 1.0, 0.0)
        cnt[s] = jnp.broadcast_to(jnp.sum(below, axis=1, keepdims=True), (16, T))

    def prepare_queries(r):
        qt[:, r * T : (r + 1) * T] = qs[r, 0:T, :].T
        gt[:, r * T : (r + 1) * T] = gs[r].T

    key_row = lax.broadcasted_iota(jnp.int32, (T, T), 0).astype(F32)
    query_lane = lax.broadcasted_iota(jnp.int32, (1, T), 1).astype(F32)
    doc_q = lax.broadcasted_iota(jnp.int32, (16, T), 0).astype(F32)

    def near_slot(r):
        own = (r == 0) | (r > z)
        used = own | ((x == X - 1) & (r >= 4))
        return used, jnp.where(own, 0, 3)

    def block_lanes(r):
        return pl.ds(pl.multiple_of(r * T, T), T)

    def piece(blocks, which, chunks, diagonal=False):
        tops, lows = [], []
        for n, r in enumerate(blocks):
            seg = qs[r, T : T + SEG_ROWS, :].astype(F32)
            same = jnp.concatenate([seg[0:1, :], seg[1:2, :]], axis=1) == doc_q
            low = [jnp.sum(jnp.where(same, cnt[s], 0.0), axis=0, keepdims=True) for _, s in chunks]
            lows.append([jnp.where(x >= 2, v, 1e9) if u == 2 else v for v, (u, _) in zip(low, chunks)])
            tops.append(run[0:1, block_lanes(r)])
        parts = [(i, s, c, u * C + c * T) for i, (u, s) in enumerate(chunks) for c in range(2)]
        for b, (i, s, c, row) in enumerate(parts):
            for n, r in enumerate(blocks):
                sc = dot_nt(ks[s, c, 0:T, :], qs[r, 0:T, :])
                allowed = key_row >= lows[n][i] - c * T
                if diagonal:
                    allowed = allowed & (key_row <= query_lane + ((core - c) * T).astype(F32))
                sc = jnp.where(allowed, sc, NEG)
                sbuf[n, b] = sc
                tops[n] = jnp.maximum(tops[n], jnp.max(sc, axis=0, keepdims=True))
        totals = [jnp.zeros((1, T), F32) for _ in blocks]
        moments = [jnp.zeros((1, T), F32) for _ in blocks]
        for b, (i, s, c, row) in enumerate(parts):
            for n, r in enumerate(blocks):
                e = jnp.exp2((sbuf[n, b] - tops[n]) * ALPHA)
                weighted = e * dot_nt(vs[s, c], gs[r])
                eb[row : row + T, block_lanes(r)] = e.astype(BF16)
                sbuf[n, b] = e
                dbuf[n, b] = weighted
                totals[n] += jnp.sum(e, axis=0, keepdims=True)
                moments[n] += jnp.sum(weighted, axis=0, keepdims=True)
        means = [moment / jnp.maximum(total, 1e-30) for moment, total in zip(moments, totals)]
        for b, (i, s, c, row) in enumerate(parts):
            for n, r in enumerate(blocks):
                tb[row : row + T, block_lanes(r)] = (dbuf[n, b] - sbuf[n, b] * means[n]).astype(BF16)
        for n, r in enumerate(blocks):
            lanes = block_lanes(r)
            pst[which, 0:1, lanes] = tops[n]
            pst[which, 1:2, lanes] = means[n]
            keep = jnp.exp2((run[0:1, lanes] - tops[n]) * ALPHA)
            run[0:1, lanes] = tops[n]
            run[1:2, lanes] = run[1:2, lanes] * keep + totals[n]
            run[2:3, lanes] = run[2:3, lanes] * keep + moments[n]

    def near_products(r, s):
        lanes = block_lanes(r)
        keys = pl.ds(pl.multiple_of(s * C, C), C)
        part_v = dot(vkt[:, keys], eb[0:C, lanes])
        part_t = dot(vkt[HD:, keys], tb[0:C, lanes])
        accv[:, lanes] = part_v
        accw[:, lanes] = part_t + pst[0, 1:2, lanes] * part_v[HD:, :]

    def far_products(lanes):
        part_v = dot(vkt[:, C : 3 * C], eb[C : 3 * C, lanes])
        part_t = dot(vkt[HD:, C : 3 * C], tb[C : 3 * C, lanes])
        keep = jnp.exp2((pst[0, 0:1, lanes] - run[0:1, lanes]) * ALPHA)
        accv[:, lanes] = accv[:, lanes] * keep + part_v
        accw[:, lanes] = accw[:, lanes] * keep + part_t + pst[1, 1:2, lanes] * part_v[HD:, :]

    def near_piece(r, multiply):
        used, s = near_slot(r)

        @pl.when(used)
        def _():
            piece([r], 0, [(0, s)])
            if multiply:
                near_products(r, s)

        @pl.when(jnp.logical_not(used))
        def _():
            lanes = block_lanes(r)
            eb[0:C, lanes] = jnp.zeros((C, T), BF16)
            tb[0:C, lanes] = jnp.zeros((C, T), BF16)
            pst[0, 0:1, lanes] = jnp.full((1, T), NEG, F32)
            pst[0, 1:2, lanes] = jnp.zeros((1, T), F32)
            accv[:, lanes] = jnp.zeros((2 * HD, T), F32)
            accw[:, lanes] = jnp.zeros((HD, T), F32)

    lane_block = lax.broadcasted_iota(jnp.int32, (1, Z * T), 1) // T
    own_lanes = (lane_block == 0) | (lane_block > z)
    upper = slice(4 * T, Z * T)

    def pack(i, values):
        for n in range(3):
            for h in range(2):
                sto[i, 2 * n + h : 2 * n + h + 1, :] = values[n][:, h * HD : (h + 1) * HD]

    def merge(parts):
        top = functools.reduce(jnp.maximum, [p[0:2, :] for p in parts])
        scales = [jnp.exp2((p[0:2, :] - top) * ALPHA) for p in parts]
        total = sum(p[2:4, :] * scale for p, scale in zip(parts, scales))
        moment = sum(p[4:6, :] * scale for p, scale in zip(parts, scales))
        return top, total, moment

    def stat_send(r):
        return copy(sto.at[r], sti.at[32 + r], st_s.at[r], st_r.at[r], dev(x, z - r, core))

    far_blocks = (3, 5, 4)

    def total_send(kind, d):
        r = 0 if kind == 0 else far_blocks[kind - 1]
        slot = kind * Z + (d + r) % Z
        return copy(sto.at[r], sti.at[slot], fn_s.at[0], fn_r.at[0], dev(x, z + d, core))

    prepare_queries(0)
    k_sib[0].wait_recv()
    v_sib[0].wait_recv()
    prepare_keys(0)
    piece([0], 0, [(0, 0)], diagonal=True)
    near_products(0, 0)

    z_step(1, 0)
    k_right.wait_recv()
    k_far.start()
    k_sib[1].start()
    v_left.wait_recv()
    v_far.start()
    v_sib[3].start()
    z_step(1, 1)
    v_right.wait_recv()
    v_sib[1].start()
    k_left.wait_recv()
    k_sib[3].start()
    prepare_queries(1)
    prepare_queries(7)
    z_step(2, 0)
    for s in (1, 3):
        k_sib[s].wait_recv()
        v_sib[s].wait_recv()
        prepare_keys(s)

    def early(i, _):
        @pl.when(i == 1)
        def _():
            k_far.wait_recv()
            k_sib[2].start()
            v_far.wait_recv()
            v_sib[2].start()

        @pl.when(i == 2)
        def _():
            z_step(2, 1)
            prepare_queries(2)
            prepare_queries(6)

        near_piece(pick(i, [1, 7, 2, 6]), True)
        return 0

    lax.fori_loop(0, 4, early, 0)
    z_step(3, 0)
    k_sib[2].wait_recv()
    v_sib[2].wait_recv()
    prepare_keys(2)

    def block(i, _):
        @pl.when(i == 2)
        def _():
            z_step(3, 1)

        r = pick(i, [0, 1, 7, 2, 6])

        @pl.when(x >= 1)
        def _():
            piece([r], 1, [(1, 1), (2, 2)])

        @pl.when(i > 0)
        def _():
            pack(r, [run[n : n + 1, block_lanes(r)] for n in range(3)])
            stat_send(r).start()

        return 0

    lax.fori_loop(0, 5, block, 0)

    def late_block(i, _):
        @pl.when(i == 2)
        def _():
            for r in (1, 7, 2, 6):
                stat_send(r).wait_recv()
            own = [run[n : n + 1, 0:T] for n in range(3)]
            pack(0, own)
            merged = merge([sto[0]] + [sti[32 + r] for r in (1, 7, 2, 6)])
            for n in range(3):
                sto[0, 2 * n : 2 * n + 2, :] = merged[n]
            for d in (3, 5, 2, 6, 1, 7):
                total_send(0, d).start()
            z_step(4, 0)
            for kind in range(3):
                total_send(kind, 4).start()

        r = pick(i, [3, 5, 4])
        near_piece(r, False)
        used, s = near_slot(r)

        @pl.when((i < 2) & used)
        def _():
            near_products(r, s)

        @pl.when(x >= 1)
        def _():
            piece([r], 1, [(1, 1), (2, 2)])

        pack(r, [run[n : n + 1, block_lanes(r)] for n in range(3)])

        for kind in (1, 2):

            @pl.when(i == kind - 1)
            def _():
                for d in (3, 5, 2, 6, 1, 7):
                    total_send(kind, d).start()

        return 0

    lax.fori_loop(0, 3, late_block, 0)
    for d in (4, 3, 5, 2, 6, 1, 7):
        total_send(3, d).start()


    used, s_zero = near_slot(4)

    @pl.when(used)
    def _():
        near_products(4, s_zero)

    @pl.when(x >= 1)
    def _():
        def body(i, _):
            far_products(pl.ds(pl.multiple_of(i * 2 * T, 2 * T), 2 * T))
            return 0

        lax.fori_loop(0, 4, body, 0)

    for r in (3, 5, 4):
        prepare_queries(r)

    pltpu.make_async_copy(
        sti.at[pl.ds(0, 4 * (Z - 1))], sti.at[pl.ds(0, 4 * (Z - 1))], fn_r.at[0]
    ).wait()
    for r in range(Z):
        parts = [sto[0] if r == 0 else sti[r]]
        for kind in (1, 2, 3):
            parts.append(sto[r] if far_blocks[kind - 1] == r else sti[kind * Z + r])
        top, total, moment = merge(parts)
        inverse = 1.0 / total
        for n, value in enumerate((top, inverse, moment * inverse)):
            fin[n : n + 1, r * T : (r + 1) * T] = jnp.concatenate([value[0:1, :], value[1:2, :]], axis=1)

    def z_sum(d, i, what, h):
        return copy(
            zs.at[d, i, what, h], zr.at[d, i, what, h], za_s.at[d, i, what, h], za_r.at[d, i, what, h],
            z_right if d == 0 else z_left,
        )

    def z_part(r, what, h):
        rows = slice(h * 128, (h + 1) * 128)
        later = slice(HD + h * 128, HD + (h + 1) * 128)
        lanes = slice(r * T, (r + 1) * T)
        scale = jnp.exp2((run[0:1, lanes] - fin[0:1, lanes]) * ALPHA) * fin[1:2, lanes]
        if what == 0:
            return accv[rows, lanes] * scale
        return (accw[rows, lanes] - fin[2:3, lanes] * accv[later, lanes]) * (scale * INV_ROOT)

    def z_add(i, order=(1, 0)):
        for short in order:
            for h in range(1):
                for d in range(2):
                    what = 1 - d if short else d
                    r = 4 + i if d == 0 else 4 - i
                    part = z_part(r, what, h)
                    if i > short:
                        z_sum(d, i - 1, what, h).wait_recv()
                        part = part + zr[d, i - 1, what, h].astype(F32)
                    zs[d, i, what, h] = part.astype(BF16)
                    send(z_sum(d, i, what, h))

    def sib_send(s):
        return copy(sbs.at[s], sbr.at[s], sb_s.at[s], sb_r.at[s], sib)

    mine = pl.ds(pl.multiple_of(core * T, T), T)
    other = pl.ds(pl.multiple_of((1 - core) * T, T), T)

    def scale_left(which, lanes, valid):
        scale = jnp.exp2((pst[which, 0:1, lanes] - fin[0:1, lanes]) * ALPHA) * fin[1:2, lanes]
        if valid is not None:
            scale = jnp.where(valid, scale, 0.0)
        root = scale * INV_ROOT
        shift = root * (pst[which, 1:2, lanes] - fin[2:3, lanes])
        q = qt[:, lanes].astype(F32)
        left_e[0:HD, lanes] = (gt[:, lanes].astype(F32) * scale).astype(BF16)
        left_e[HD:, lanes] = (q * shift).astype(BF16)
        left_t[:, lanes] = (q * root).astype(BF16)

    def sib_half(s):
        sbs[s] = kacc[s, :, other].astype(BF16)
        send(sib_send(s))

    def key_products(s, rows, lanes):
        kacc[s] = dot_nt(left_e[:, lanes], eb[rows, lanes])
        kacc[s, HD:, :] += dot_nt(left_t[:, lanes], tb[rows, lanes])

    def far_key(s):
        @pl.when(x >= s)
        def _():
            rows = slice(s * C, (s + 1) * C)
            key_products(s, rows, slice(0, Z * T))

        @pl.when(x < s)
        def _():
            kacc[s] = jnp.zeros((2 * HD, C), F32)

        sib_half(s)

    def own_part(s, what):
        rows = slice(what * HD, (what + 1) * HD)
        return kacc[s, rows, mine] + sbr[s, rows, :].astype(F32)

    x_target = [x_right, x_left, x_left, x_left, x_right, x_right]

    def x_sum(i):
        return copy(xs.at[i], xr.at[i], xr_s.at[i], xr_r.at[i], x_target[i])

    def x_send(i, part):
        xs[i] = part.astype(BF16)
        send(x_sum(i))

    z_add(0, (0,))
    z_add(1, (1,))

    @pl.when(x >= 1)
    def _():
        scale_left(1, slice(0, Z * T), None)

    far_key(2)
    far_key(1)
    sib_send(2).wait_recv()
    x_send(0, own_part(2, 0))
    x_send(1, own_part(2, 1))
    z_add(1, (0,))

    @pl.when(x == X - 1)
    def _():
        scale_left(0, upper, jnp.logical_not(own_lanes)[:, upper])
        key_products(3, slice(0, C), upper)

    @pl.when(x < X - 1)
    def _():
        kacc[3] = jnp.zeros((2 * HD, C), F32)

    sib_half(3)
    sib_send(1).wait_recv()
    x_send(2, own_part(1, 0))
    sib_send(3).wait_recv()
    x_send(5, own_part(3, 1))
    z_add(2)
    scale_left(0, slice(0, Z * T), own_lanes)
    key_products(0, slice(0, C), slice(0, Z * T))
    sib_half(0)
    x_sum(1).wait_recv()
    x_send(3, own_part(1, 1) + xr[1].astype(F32))
    x_sum(0).wait_recv()
    x_send(4, own_part(3, 0) + xr[0].astype(F32))
    z_add(3)

    def leave(i):
        return pltpu.make_async_copy(out_v.at[i], out_ref.at[i], out_s.at[i])

    sib_send(0).wait_recv()
    for what, near in ((0, (2, 4)), (1, (3, 5))):
        part = own_part(0, what)
        for i in near:
            x_sum(i).wait_recv()
            part = part + xr[i].astype(F32)
        out_v[3 - what] = part.T.astype(BF16)
        leave(3 - what).start()

    for hops in (*q_right, *q_left, *g_right, *g_left):
        for op in hops:
            op.wait_send()
    for op in (*k_sib, *v_sib, k_right, v_right, k_left, v_left, k_far, v_far):
        op.wait_send()
    for r in (1, 7, 2, 6):
        stat_send(r).wait_send()
    pltpu.make_async_copy(
        sti.at[pl.ds(0, 4 * (Z - 1))], sti.at[pl.ds(0, 4 * (Z - 1))], fn_s.at[0]
    ).wait()
    for op in started:
        op.wait_send()

    for what in range(2):
        halves = []
        for h in range(1):
            part = z_part(0, what, h)
            for d in range(2):
                z_sum(d, 3, what, h).wait_recv()
                part = part + zr[d, 3, what, h].astype(F32)
            halves.append(part)
        out_v[what] = jnp.concatenate(halves, axis=0).T.astype(BF16)
        leave(what).start()
    for i in range(4):
        leave(i).wait()


def hand_on(all_ref, *outs):
    for i, out in enumerate(outs):
        out[...] = all_ref[i]


def per_device(queries, keys, values, out_grad, segments):
    place = pl.BlockSpec(memory_space=pl.ANY)
    vmem = pl.BlockSpec(memory_space=pltpu.VMEM)
    dma = pltpu.SemaphoreType.DMA
    sums = pl.pallas_call(
        kernel,
        out_shape=jax.ShapeDtypeStruct((4, T, HD), BF16),
        in_specs=[place] * 5,
        out_specs=place,
        scratch_shapes=[
            pltpu.VMEM((T // HD, HD), jnp.int32),
            pltpu.VMEM((SEG_ROWS, HD), F32),
            pltpu.VMEM((4, T, HD), BF16),
            pltpu.VMEM((Z, T + SEG_ROWS, HD), BF16),
            pltpu.VMEM((Z, T, HD), BF16),
            pltpu.VMEM((HD, Z * T), BF16),
            pltpu.VMEM((HD, Z * T), BF16),
            pltpu.VMEM((X, 2, T + SEG_ROWS, HD), BF16),
            pltpu.VMEM((X, 2, T, HD), BF16),
            pltpu.VMEM((2 * HD, X * C), BF16),
            pltpu.VMEM((3 * C, Z * T), BF16),
            pltpu.VMEM((3 * C, Z * T), BF16),
            pltpu.VMEM((2, 4, T, T), F32),
            pltpu.VMEM((2, 4, T, T), F32),
            pltpu.VMEM((2, 8, Z * T), F32),
            pltpu.VMEM((8, Z * T), F32),
            pltpu.VMEM((2 * HD, Z * T), F32),
            pltpu.VMEM((HD, Z * T), F32),
            pltpu.VMEM((2 * HD, Z * T), BF16),
            pltpu.VMEM((HD, Z * T), BF16),
            pltpu.VMEM((X, 2 * HD, C), F32),
            pltpu.VMEM((X, 16, T), F32),
            pltpu.VMEM((Z, 8, HD), F32),
            pltpu.VMEM((5 * Z, 8, HD), F32),
            pltpu.VMEM((8, Z * T), F32),
            pltpu.VMEM((2, 4, 2, 1, HD // 1, T), BF16),
            pltpu.VMEM((2, 4, 2, 1, HD // 1, T), BF16),
            pltpu.VMEM((X, 2 * HD, T), BF16),
            pltpu.VMEM((X, 2 * HD, T), BF16),
            pltpu.VMEM((6, HD, T), BF16),
            pltpu.VMEM((6, HD, T), BF16),
            dma((Z, 1)), dma((Z, 1)), dma((Z, 1)), dma((Z, 1)),
            dma((14,)), dma((14,)),
            dma((Z,)), dma((Z,)), dma((1,)), dma((1,)),
            dma((2, 4, 2, 1)), dma((2, 4, 2, 1)),
            dma((X,)), dma((X,)), dma((6,)), dma((6,)), dma((5,)), dma((4,)),
        ],
        compiler_params=pltpu.CompilerParams(
            collective_id=0, has_side_effects=True, vmem_limit_bytes=58 * 1024 * 1024
        ),
        cost_estimate=pl.CostEstimate(
            flops=4 * 10**9, bytes_accessed=600_000, transcendentals=2 * 10**6
        ),
    )(queries, keys, values, out_grad, segments.reshape(T // HD, HD))
    return tuple(sums[i] for i in range(4))


def solution(mesh):
    rows = P(("dp", "ctx"), None)
    return jax.shard_map(
        per_device,
        mesh=mesh,
        in_specs=(rows, rows, rows, rows, P(("dp", "ctx"))),
        out_specs=(rows, rows, rows, rows),
        check_vma=False,
    )
```

time: 51.4 us -> 50.5 us (0.982)
  Pallas kernels: 50.6 us -> 47.8 us
  local copies, waits for them, and re-layouts: 0 us -> 1.64 us
    pallas_call x1 -> x0, Pallas kernels: 1.65 us -> none  [per_device(): pl.pallas_call(hand_on, out_shape=(jax.ShapeDtypeStruct((T, HD), BF16),)...]
    squeeze x0 -> x1, local copies, waits for them, and re-layouts: none -> 1.64 us  [per_device(): return tuple((sums[i] for i in range(4)))]
    pallas_call x1, Pallas kernels: 49 us -> 47.8 us  [per_device(): pl.pallas_call(kernel, out_shape=jax.ShapeDtypeStruct((4, T, HD), BF16),...]
where the time goes in v5:
time: 50.5 us; the launch traced here: 50.1 us
  Pallas kernels  47.8 us (95%)
  local copies, waits for them, and re-layouts  1.64 us (3%)
  between operations  0.64 us (1%)
    pallas_call x1, Pallas kernels, per_device(): pl.pallas_call(kernel, out_shape=jax.ShapeDtypeStruct((4, T, HD), BF16),...  47.8 us
    squeeze x1, local copies, waits for them, and re-layouts, per_device(): return tuple((sums[i] for i in range(4)))  1.64 us

profile of v5, /device:TPU:8, one launch (start us, length us, event | category | flops | bytes accessed | tf_op | source)
XLA Modules:
  0.0 50.1 jit_solution(12274007507038011933)
XLA Ops:
  0.6 47.8 %shard_map.84 = bf16[4,256,128]{2,1,0:T(8,128)(2,1)} custom-call(bf16[256,128]{1,0:T(8,128)(2,1)} %q_ref.1, bf16[256,128]{1,0:T(8,128)(2,1)} %k_ref.1, bf16[256,128]{1,0:T(8,128)(2,1)} %v_ref.1, bf16[256,128]{1,0:T(8,128)(2,1)} %g_ref.1, s32[2,128]{1,0:T(2,128)} %bitcast.9), custom_call_target="tpu_custom_call" | custom-call | flops 4000000000 | bytes 600000 | tf_op jit(solution)/shard_map/pallas_call | solution.py:584
  48.5 1.6 %slice_bitcast_fusion = (bf16[256,128]{1,0:T(8,128)(2,1)}, bf16[256,128]{1,0:T(8,128)(2,1)}, bf16[256,128]{1,0:T(8,128)(2,1)}, bf16[256,128]{1,0:T(8,128)(2,1)}) fusion(bf16[4,256,128]{2,1,0:T(8,128)(2,1)} %shard_map.84), kind=kLoop, calls=%fused_computation | loop fusion | bytes 524288 | tf_op jit(solution)/shard_map/squeeze | solution.py:634

commit v6 on v5

--- a/solution.py
+++ b/solution.py
@@ -402,8 +402,6 @@
 
         lax.fori_loop(0, 4, body, 0)
 
-    for r in (3, 5, 4):
-        prepare_queries(r)
 
     pltpu.make_async_copy(
         sti.at[pl.ds(0, 4 * (Z - 1))], sti.at[pl.ds(0, 4 * (Z - 1))], fn_r.at[0]
@@ -497,6 +495,8 @@
 
     z_add(0, (0,))
     z_add(1, (1,))
+    for r in (3, 5, 4):
+        prepare_queries(r)
 
     @pl.when(x >= 1)
     def _():

time: 50.5 us -> 50.7 us (level)
  no operation moved by 1% of the time
where the time goes in v6:
time: 50.7 us; the launch traced here: 50.1 us
  Pallas kernels  47.8 us (94%)
  local copies, waits for them, and re-layouts  1.64 us (3%)
  between operations  0.64 us (1%)
    pallas_call x1, Pallas kernels, per_device(): pl.pallas_call(kernel, out_shape=jax.ShapeDtypeStruct((4, T, HD), BF16),...  47.8 us
    squeeze x1, local copies, waits for them, and re-layouts, per_device(): return tuple((sums[i] for i in range(4)))  1.64 us

profile of v6, /device:TPU:8, one launch (start us, length us, event | category | flops | bytes accessed | tf_op | source)
XLA Modules:
  0.0 50.1 jit_solution(2551406870578934896)
XLA Ops:
  0.6 47.8 %shard_map.84 = bf16[4,256,128]{2,1,0:T(8,128)(2,1)} custom-call(bf16[256,128]{1,0:T(8,128)(2,1)} %q_ref.1, bf16[256,128]{1,0:T(8,128)(2,1)} %k_ref.1, bf16[256,128]{1,0:T(8,128)(2,1)} %v_ref.1, bf16[256,128]{1,0:T(8,128)(2,1)} %g_ref.1, s32[2,128]{1,0:T(2,128)} %bitcast.9), custom_call_target="tpu_custom_call" | custom-call | flops 4000000000 | bytes 600000 | tf_op jit(solution)/shard_map/pallas_call | solution.py:584
  48.5 1.6 %slice_bitcast_fusion = (bf16[256,128]{1,0:T(8,128)(2,1)}, bf16[256,128]{1,0:T(8,128)(2,1)}, bf16[256,128]{1,0:T(8,128)(2,1)}, bf16[256,128]{1,0:T(8,128)(2,1)}) fusion(bf16[4,256,128]{2,1,0:T(8,128)(2,1)} %shard_map.84), kind=kLoop, calls=%fused_computation | loop fusion | bytes 524288 | tf_op jit(solution)/shard_map/squeeze | solution.py:634

commit v7 on v5

--- a/solution.py
+++ b/solution.py
@@ -325,10 +325,6 @@
     prepare_keys(2)
 
     def block(i, _):
-        @pl.when(i == 2)
-        def _():
-            z_step(3, 1)
-
         r = pick(i, [0, 1, 7, 2, 6])
 
         @pl.when(x >= 1)
@@ -343,6 +339,7 @@
         return 0
 
     lax.fori_loop(0, 5, block, 0)
+    z_step(3, 1)
 
     def late_block(i, _):
         @pl.when(i == 2)

time: 50.5 us -> 50.2 us (level)
  Pallas kernels: 47.8 us -> 47.2 us
    pallas_call x1, Pallas kernels: 47.8 us -> 47.2 us  [per_device(): pl.pallas_call(kernel, out_shape=jax.ShapeDtypeStruct((4, T, HD), BF16),...]
where the time goes in v7:
time: 50.2 us; the launch traced here: 49.5 us
  Pallas kernels  47.2 us (94%)
  local copies, waits for them, and re-layouts  1.64 us (3%)
  between operations  0.64 us (1%)
    pallas_call x1, Pallas kernels, per_device(): pl.pallas_call(kernel, out_shape=jax.ShapeDtypeStruct((4, T, HD), BF16),...  47.2 us
    squeeze x1, local copies, waits for them, and re-layouts, per_device(): return tuple((sums[i] for i in range(4)))  1.64 us

profile of v7, /device:TPU:8, one launch (start us, length us, event | category | flops | bytes accessed | tf_op | source)
XLA Modules:
  0.0 49.5 jit_solution(11079420752602775099)
XLA Ops:
  0.6 47.2 %shard_map.84 = bf16[4,256,128]{2,1,0:T(8,128)(2,1)} custom-call(bf16[256,128]{1,0:T(8,128)(2,1)} %q_ref.1, bf16[256,128]{1,0:T(8,128)(2,1)} %k_ref.1, bf16[256,128]{1,0:T(8,128)(2,1)} %v_ref.1, bf16[256,128]{1,0:T(8,128)(2,1)} %g_ref.1, s32[2,128]{1,0:T(2,128)} %bitcast.9), custom_call_target="tpu_custom_call" | custom-call | flops 4000000000 | bytes 600000 | tf_op jit(solution)/shard_map/pallas_call | solution.py:581
  47.9 1.6 %slice_bitcast_fusion = (bf16[256,128]{1,0:T(8,128)(2,1)}, bf16[256,128]{1,0:T(8,128)(2,1)}, bf16[256,128]{1,0:T(8,128)(2,1)}, bf16[256,128]{1,0:T(8,128)(2,1)}) fusion(bf16[4,256,128]{2,1,0:T(8,128)(2,1)} %shard_map.84), kind=kLoop, calls=%fused_computation | loop fusion | bytes 524288 | tf_op jit(solution)/shard_map/squeeze | solution.py:631
